TPU v7x, 128 devices: a whole 4x4x4 slice. The times are simulated.
128 devices in a mesh: dp: 16 (over y, x), expert: 8 (over z, core).
Axes of the slice: x: 4, y: 4, z: 4, core: 2. Of those that a mesh axis runs over, the one named last changes fastest.
Arguments:
- tokens: bfloat16 [32768, 1024], P(('dp', 'expert'))
- cotangent: bfloat16 [32768, 1024], P(('dp', 'expert')), may hold values from -6 to 6
- routes: int32 [32768, 4], P(('dp', 'expert')), may hold values from 0 to 31, as said below
- slot_ids: int32 [32768, 4], P(('dp', 'expert')), may hold values from 0 to 63, as said below
- attn_gain: float32 [1024], replicated, may hold values from 0.25 to 1.75
- w_qkv: bfloat16 [1024, 2048], replicated, may hold values from -0.1875 to 0.1875
- b_qkv: float32 [2048], replicated, may hold values from -0.6 to 0.6
- w_out: bfloat16 [1024, 1024], replicated, may hold values from -0.75 to 0.75
- b_out: float32 [1024], replicated, may hold values from -0.6 to 0.6
- sink_logits: float32 [16], replicated, may hold values from 1 to 5
- moe_gain: float32 [1024], replicated, may hold values from 0.25 to 1.75
- w_router: bfloat16 [1024, 32], replicated, may hold values from -0.09375 to 0.09375
- b_router: float32 [32], replicated, may hold values from -1.5 to 1.5
- gu_weight: bfloat16 [32, 512, 2, 1024], P('expert', 'dp'), may hold values from -0.1875 to 0.1875
- gu_bias: float32 [32, 2, 512], P('expert'), may hold values from -0.6 to 0.6
- down_weight: bfloat16 [32, 512, 1024], P('expert', 'dp'), may hold values from -0.25 to 0.25
- down_bias: float32 [32, 1024], replicated, may hold values from -0.6 to 0.6
Outputs:
- block_out: bfloat16 [32768, 1024], P(('dp', 'expert'))
- d_tokens: bfloat16 [32768, 1024], P(('dp', 'expert'))
- d_attn_gain: float32 [1024], replicated
- d_w_qkv: float32 [1024, 2048], replicated
- d_b_qkv: float32 [2048], replicated
- d_w_out: float32 [1024, 1024], replicated
- d_b_out: float32 [1024], replicated
- d_sink_logits: float32 [16], replicated
- d_moe_gain: float32 [1024], replicated
- d_w_router: float32 [1024, 32], replicated
- d_b_router: float32 [32], replicated
- d_gu_weight: float32 [32, 512, 2, 1024], P('expert', 'dp')
- d_gu_bias: float32 [32, 2, 512], P('expert', None, 'dp')
- d_down_weight: float32 [32, 512, 1024], P('expert', 'dp')
- d_down_bias: float32 [32, 1024], replicated
Inputs may be any that keep to these rules, and one draw needn't show every extreme that they name: `routes`: each row names 4 different experts. Among the 256 rows of one device each expert is named at most 64 times. On the devices that hold one sequence (8 devices in a row) one expert is named exactly 64 times on every device, and on each device a second expert too. `slot_ids`: among the rows of one device, the (row, choice) pairs that name one expert have distinct slot numbers.
All inputs are finite; a program needn't handle non-finite values.
Results may differ from a plain program's by a relative error of at most 0.015.
Values may be sent and summed in bfloat16 or wider, within the bound.
A program may use at most 192 MiB of HBM per device.

v0:
```python
import jax
import jax.numpy as jnp
from jax import lax
from jax.sharding import PartitionSpec as P

FF = 512
HEADS = 16
KV_HEADS = 8
HEAD_DIM = 64


EPS = 1e-05
THETA = 10000.0
LIMIT = 7.0
ALPHA = 1.702
NEG = -1000000000.0
HIGH = lax.Precision.HIGHEST


def rotate(values_in, places, direction):
    half_dim = values_in.shape[-1] // 2
    frequency = jnp.exp(
        jnp.arange(half_dim, dtype=jnp.float32) * (-2.0 * jnp.log(THETA) / values_in.shape[-1])
    )
    angles = places.astype(jnp.float32)[:, None] * frequency[None, :]
    cosine = jnp.cos(angles)[:, None, :]
    sine_part = direction * jnp.sin(angles)[:, None, :]
    first_half = values_in[..., :half_dim]
    second = values_in[..., half_dim:]
    return jnp.concatenate(
        [first_half * cosine - second * sine_part, second * cosine + first_half * sine_part],
        axis=-1,
    )


def norm_forward(stream, norm_gain):
    inverse = lax.rsqrt(jnp.mean(stream * stream, axis=-1, keepdims=True) + EPS)
    return (stream * inverse * norm_gain, inverse)


def norm_backward(stream, inverse, norm_gain, grad_out):
    weighted = grad_out * norm_gain
    inner_mean = jnp.mean(weighted * stream, axis=-1, keepdims=True)
    grad_in = inverse * weighted - stream * inverse * inverse * inverse * inner_mean
    grad_gain = jnp.sum(grad_out * stream * inverse, axis=0)
    return (grad_in, grad_gain)


def swiglu(gate_pre, up_pre):
    gate_clip = LIMIT * jnp.tanh(gate_pre / LIMIT)
    up_clip = LIMIT * jnp.tanh(up_pre / LIMIT)
    return (up_clip + 1.0) * gate_clip * jax.nn.sigmoid(ALPHA * gate_clip)


def swiglu_back(gate_pre, up_pre, grad_out):
    gate_clip = LIMIT * jnp.tanh(gate_pre / LIMIT)
    up_clip = LIMIT * jnp.tanh(up_pre / LIMIT)
    sigmoid_gate = jax.nn.sigmoid(ALPHA * gate_clip)
    glu_value = gate_clip * sigmoid_gate
    glu_slope = sigmoid_gate + ALPHA * gate_clip * sigmoid_gate * (1.0 - sigmoid_gate)
    gate_ratio = gate_clip / LIMIT
    up_ratio = up_clip / LIMIT
    grad_gate = grad_out * (up_clip + 1.0) * glu_slope * (1.0 - gate_ratio * gate_ratio)
    grad_up = grad_out * glu_value * (1.0 - up_ratio * up_ratio)
    return (grad_gate, grad_up)


def per_device(
    tokens,
    cotangent,
    routes,
    slot_ids,
    attn_gain,
    w_qkv,
    b_qkv,
    w_out,
    b_out,
    sink_logits,
    moe_gain,
    w_router,
    b_router,
    gu_weight,
    gu_bias,
    down_weight,
    down_bias,
):
    row_count = tokens.shape[0]
    model_width = tokens.shape[1]
    groups = lax.axis_size("expert")
    length = row_count * groups
    experts = w_router.shape[1]
    exp_local = gu_weight.shape[0]
    ff_local = gu_weight.shape[1]
    top_count = routes.shape[1]
    capacity = 2 * row_count * top_count // experts
    n_query = HEADS * HEAD_DIM
    n_key = KV_HEADS * HEAD_DIM
    repeat = HEADS // KV_HEADS
    scale_qk = HEAD_DIM ** (-0.5)
    owner_index = lax.axis_index("expert")
    places = owner_index * row_count + jnp.arange(row_count, dtype=jnp.int32)
    key_places = jnp.arange(length, dtype=jnp.int32)
    row_places = jnp.tile(places, repeat)
    allowed = row_places[:, None] >= key_places[None, :]
    stream = tokens.astype(jnp.float32)
    normed, inverse_one = norm_forward(stream, attn_gain)
    normed_low = normed.astype(jnp.bfloat16)
    qkv_mixed = jnp.dot(normed_low, w_qkv, preferred_element_type=jnp.float32) + b_qkv
    queries = rotate(
        qkv_mixed[:, :n_query].reshape(row_count, HEADS, HEAD_DIM), places, 1.0
    ).astype(jnp.bfloat16)
    key_own = rotate(
        qkv_mixed[:, n_query : n_query + n_key].reshape(row_count, KV_HEADS, HEAD_DIM), places, 1.0
    ).astype(jnp.bfloat16)
    value_own = qkv_mixed[:, n_query + n_key :].astype(jnp.bfloat16)
    key_all, value_all = (
        lax.all_gather(key_own.reshape(row_count, n_key), "expert", axis=0, tiled=True),
        lax.all_gather(value_own, "expert", axis=0, tiled=True),
    )
    query_heads = (
        queries.reshape(row_count, KV_HEADS, repeat, HEAD_DIM)
        .transpose(1, 2, 0, 3)
        .reshape(KV_HEADS, repeat * row_count, HEAD_DIM)
    )
    key_heads = key_all.reshape(length, KV_HEADS, HEAD_DIM).transpose(1, 0, 2)
    value_heads = value_all.reshape(length, KV_HEADS, HEAD_DIM).transpose(1, 0, 2)
    sink_rows = jnp.repeat(sink_logits.reshape(KV_HEADS, repeat), row_count, axis=1)

    def head_scores(query_part, key_part):
        scores = (
            jnp.einsum("qd,kd->qk", query_part, key_part, preferred_element_type=jnp.float32)
            * scale_qk
        )
        return jnp.where(allowed, scores, NEG)

    def attend_head(operands):
        query_part, key_part, value_part, sink_part = operands
        scores = head_scores(query_part, key_part)
        row_max = jnp.maximum(jnp.max(scores, axis=-1), sink_part)
        exp_scores = jnp.exp(scores - row_max[:, None])
        row_total = jnp.sum(exp_scores, axis=-1) + jnp.exp(sink_part - row_max)
        weights_low = (exp_scores / row_total[:, None]).astype(jnp.bfloat16)
        attended_part = jnp.einsum(
            "qk,kd->qd", weights_low, value_part, preferred_element_type=jnp.float32
        )
        return (attended_part.astype(jnp.bfloat16), row_max + jnp.log(row_total))

    attended_heads, log_totals = lax.map(
        attend_head, (query_heads, key_heads, value_heads, sink_rows)
    )
    attended = (
        attended_heads.reshape(KV_HEADS, repeat, row_count, HEAD_DIM)
        .transpose(2, 0, 1, 3)
        .reshape(row_count, n_query)
    )
    branch = jnp.dot(attended, w_out, preferred_element_type=jnp.float32) + b_out
    middle = stream + branch
    routed, inverse_two = norm_forward(middle, moe_gain)
    routed_low = routed.astype(jnp.bfloat16)
    logits = jnp.dot(routed_low, w_router, preferred_element_type=jnp.float32) + b_router
    gate_weights = jax.nn.softmax(jnp.take_along_axis(logits, routes, axis=1), axis=-1)
    target = (routes * capacity + slot_ids).reshape(-1)
    send_rows = (
        jnp.zeros((experts * capacity, model_width), jnp.bfloat16)
        .at[target]
        .set(jnp.repeat(routed_low, top_count, axis=0))
    )
    received = lax.all_to_all(
        send_rows.reshape(groups, exp_local, capacity, model_width),
        "expert",
        split_axis=0,
        concat_axis=0,
        tiled=True,
    )
    local_bias = lax.dynamic_slice_in_dim(down_bias, owner_index * exp_local, exp_local, 0)

    def pre_activation(gu_piece):
        gate_pre = (
            jnp.einsum(
                "secd,efd->secf", received, gu_piece[:, :, 0, :], preferred_element_type=jnp.float32
            )
            + gu_bias[None, :, None, 0, :]
        )
        up_pre = (
            jnp.einsum(
                "secd,efd->secf", received, gu_piece[:, :, 1, :], preferred_element_type=jnp.float32
            )
            + gu_bias[None, :, None, 1, :]
        )
        return (gate_pre, up_pre)

    gu_piece = lax.all_gather(gu_weight, "dp", axis=1, tiled=True)
    down_piece = lax.all_gather(down_weight, "dp", axis=1, tiled=True)
    gate_pre, up_pre = pre_activation(gu_piece)
    active = swiglu(gate_pre, up_pre).astype(jnp.bfloat16)
    expert_sum = jnp.einsum(
        "secf,efd->secd", active, down_piece, preferred_element_type=jnp.float32
    )
    expert_out = (expert_sum + local_bias[None, :, None, :]).astype(jnp.bfloat16)
    returned = lax.all_to_all(
        expert_out, "expert", split_axis=0, concat_axis=0, tiled=True
    ).reshape(experts * capacity, model_width)
    picked = returned[target].reshape(row_count, top_count, model_width).astype(jnp.float32)
    mixture = jnp.sum(gate_weights[:, :, None] * picked, axis=1)
    block_out = (middle + mixture).astype(jnp.bfloat16)
    grad_out = cotangent.astype(jnp.float32)
    grad_rows = (gate_weights[:, :, None] * grad_out[:, None, :]).astype(jnp.bfloat16)
    send_grad = (
        jnp.zeros((experts * capacity, model_width), jnp.bfloat16)
        .at[target]
        .set(grad_rows.reshape(-1, model_width))
    )
    down_bias_part = jnp.sum(
        send_grad.reshape(experts, capacity, model_width), axis=1, dtype=jnp.float32
    )
    grad_in = lax.all_to_all(
        send_grad.reshape(groups, exp_local, capacity, model_width),
        "expert",
        split_axis=0,
        concat_axis=0,
        tiled=True,
    )
    gu_piece = lax.all_gather(gu_weight, "dp", axis=1, tiled=True)
    down_piece = lax.all_gather(down_weight, "dp", axis=1, tiled=True)
    gate_pre, up_pre = pre_activation(gu_piece)
    active = swiglu(gate_pre, up_pre).astype(jnp.bfloat16)
    grad_active = jnp.einsum(
        "secd,efd->secf", grad_in, down_piece, preferred_element_type=jnp.float32
    )
    grad_gate, grad_up = swiglu_back(gate_pre, up_pre, grad_active)
    grad_gate = grad_gate.astype(jnp.bfloat16)
    grad_up = grad_up.astype(jnp.bfloat16)
    rows_grad = jnp.einsum(
        "secf,efd->secd", grad_gate, gu_piece[:, :, 0, :], preferred_element_type=jnp.float32
    ) + jnp.einsum(
        "secf,efd->secd", grad_up, gu_piece[:, :, 1, :], preferred_element_type=jnp.float32
    )
    gate_grads = grad_gate
    up_grads = grad_up
    actives = active
    back_state = (rows_grad, gate_grads, up_grads, actives)
    rows_grad, gate_grads, up_grads, actives = back_state
    bias_term = jnp.stack(
        [
            jnp.sum(gate_grads, axis=(0, 2), dtype=jnp.float32),
            jnp.sum(up_grads, axis=(0, 2), dtype=jnp.float32),
        ],
        axis=1,
    )
    bias_spread = lax.dynamic_update_slice_in_dim(
        jnp.zeros((experts, 2, FF), jnp.float32), bias_term, owner_index * exp_local, 0
    )
    gu_term = jnp.stack(
        [
            jnp.einsum("secf,secd->efd", gate_grads, received, preferred_element_type=jnp.float32),
            jnp.einsum("secf,secd->efd", up_grads, received, preferred_element_type=jnp.float32),
        ],
        axis=2,
    )
    down_term = jnp.einsum("secf,secd->efd", actives, grad_in, preferred_element_type=jnp.float32)
    d_gu_weight, d_down_weight = (
        lax.psum_scatter(
            gu_term.astype(jnp.bfloat16), "dp", scatter_dimension=1, tiled=True
        ).astype(jnp.float32),
        lax.psum_scatter(
            down_term.astype(jnp.bfloat16), "dp", scatter_dimension=1, tiled=True
        ).astype(jnp.float32),
    )
    back_rows = lax.all_to_all(
        rows_grad.astype(jnp.bfloat16), "expert", split_axis=0, concat_axis=0, tiled=True
    ).reshape(experts * capacity, model_width)
    routed_grad = jnp.sum(
        back_rows[target].reshape(row_count, top_count, model_width).astype(jnp.float32), axis=1
    )
    gate_grad = jnp.sum(picked * grad_out[:, None, :], axis=-1)
    chosen_grad = gate_weights * (
        gate_grad - jnp.sum(gate_weights * gate_grad, axis=-1, keepdims=True)
    )
    one_hot = (routes[:, :, None] == jnp.arange(experts, dtype=jnp.int32)[None, None, :]).astype(
        jnp.float32
    )
    logit_grad = jnp.einsum("tk,tke->te", chosen_grad, one_hot, precision=HIGH)
    d_w_router = jnp.einsum("td,te->de", routed_low.astype(jnp.float32), logit_grad, precision=HIGH)
    d_b_router = jnp.sum(logit_grad, axis=0)
    routed_grad = routed_grad + jnp.einsum(
        "te,de->td", logit_grad, w_router.astype(jnp.float32), precision=HIGH
    )
    middle_norm_grad, d_moe_gain = norm_backward(middle, inverse_two, moe_gain, routed_grad)
    middle_grad = grad_out + middle_norm_grad
    branch_grad = middle_grad.astype(jnp.bfloat16)
    d_b_out = jnp.sum(branch_grad, axis=0, dtype=jnp.float32)
    d_w_out = jnp.einsum("tq,td->qd", attended, branch_grad, preferred_element_type=jnp.float32)
    attended_grad = jnp.einsum(
        "td,qd->tq", branch_grad, w_out, preferred_element_type=jnp.float32
    ).astype(jnp.bfloat16)
    grad_heads = (
        attended_grad.reshape(row_count, KV_HEADS, repeat, HEAD_DIM)
        .transpose(1, 2, 0, 3)
        .reshape(KV_HEADS, repeat * row_count, HEAD_DIM)
    )

    def attend_back(operands):
        query_part, key_part, value_part, grad_part, total_part, sink_part = operands
        scores = head_scores(query_part, key_part)
        prob_rows = jnp.exp(scores - total_part[:, None])
        prob_grad = jnp.einsum(
            "qd,kd->qk", grad_part, value_part, preferred_element_type=jnp.float32
        )
        value_grad = jnp.einsum(
            "qk,qd->kd",
            prob_rows.astype(jnp.bfloat16),
            grad_part,
            preferred_element_type=jnp.float32,
        )
        inner_sum = jnp.sum(prob_rows * prob_grad, axis=-1)
        score_grad = (prob_rows * (prob_grad - inner_sum[:, None])).astype(jnp.bfloat16)
        query_grad = (
            jnp.einsum("qk,kd->qd", score_grad, key_part, preferred_element_type=jnp.float32)
            * scale_qk
        )
        key_grad = (
            jnp.einsum("qk,qd->kd", score_grad, query_part, preferred_element_type=jnp.float32)
            * scale_qk
        )
        sink_grad = -jnp.exp(sink_part - total_part) * inner_sum
        return (query_grad, key_grad, value_grad, sink_grad)

    query_grads, key_grads, value_grads, sink_grads = lax.map(
        attend_back, (query_heads, key_heads, value_heads, grad_heads, log_totals, sink_rows)
    )
    key_full = key_grads.transpose(1, 0, 2).reshape(length, n_key)
    value_full = value_grads.transpose(1, 0, 2).reshape(length, n_key)
    key_mine, value_mine = (
        lax.psum_scatter(
            key_full.astype(jnp.bfloat16), "expert", scatter_dimension=0, tiled=True
        ).astype(jnp.float32),
        lax.psum_scatter(
            value_full.astype(jnp.bfloat16), "expert", scatter_dimension=0, tiled=True
        ).astype(jnp.float32),
    )
    query_back = rotate(
        query_grads.reshape(KV_HEADS, repeat, row_count, HEAD_DIM)
        .transpose(2, 0, 1, 3)
        .reshape(row_count, HEADS, HEAD_DIM),
        places,
        -1.0,
    )
    key_back = rotate(key_mine.reshape(row_count, KV_HEADS, HEAD_DIM), places, -1.0)
    qkv_grad = jnp.concatenate(
        [query_back.reshape(row_count, n_query), key_back.reshape(row_count, n_key), value_mine],
        axis=1,
    ).astype(jnp.bfloat16)
    d_b_qkv = jnp.sum(qkv_grad, axis=0, dtype=jnp.float32)
    d_w_qkv = jnp.einsum("td,tq->dq", normed_low, qkv_grad, preferred_element_type=jnp.float32)
    normed_grad = jnp.einsum("tq,dq->td", qkv_grad, w_qkv, preferred_element_type=jnp.float32)
    stream_grad, d_attn_gain = norm_backward(stream, inverse_one, attn_gain, normed_grad)
    d_tokens = (middle_grad + stream_grad).astype(jnp.bfloat16)
    d_sinks = jnp.sum(sink_grads.reshape(KV_HEADS, repeat, row_count), axis=-1).reshape(HEADS)
    summed = lax.psum(
        (
            d_attn_gain,
            d_w_qkv,
            d_b_qkv,
            d_w_out,
            d_b_out,
            d_sinks,
            d_moe_gain,
            d_w_router,
            d_b_router,
            down_bias_part,
            bias_spread,
        ),
        ("dp", "expert"),
    )
    bias_mine = lax.dynamic_slice_in_dim(summed[10], owner_index * exp_local, exp_local, 0)
    d_gu_bias = lax.dynamic_slice_in_dim(bias_mine, lax.axis_index("dp") * ff_local, ff_local, 2)
    return (
        block_out,
        d_tokens,
        summed[0],
        summed[1],
        summed[2],
        summed[3],
        summed[4],
        summed[5],
        summed[6],
        summed[7],
        summed[8],
        d_gu_weight,
        d_gu_bias,
        d_down_weight,
        summed[9],
    )


def solution(mesh):
    in_specs = (
        P(("dp", "expert"), None),
        P(("dp", "expert"), None),
        P(("dp", "expert"), None),
        P(("dp", "expert"), None),
        P(),
        P(),
        P(),
        P(),
        P(),
        P(),
        P(),
        P(),
        P(),
        P("expert", "dp", None, None),
        P("expert", None, None),
        P("expert", "dp", None),
        P(),
    )
    out_specs = (
        P(("dp", "expert"), None),
        P(("dp", "expert"), None),
        P(),
        P(),
        P(),
        P(),
        P(),
        P(),
        P(),
        P(),
        P(),
        P("expert", "dp", None, None),
        P("expert", None, "dp"),
        P("expert", "dp", None),
        P(),
    )
    return jax.shard_map(
        per_device, mesh=mesh, in_specs=in_specs, out_specs=out_specs, check_vma=False
    )
```

profile of v0, /device:TPU:1, one launch (start us, length us, event | category | flops | bytes accessed | tf_op | source)
XLA Modules:
  0.0 992.2 jit_solution(14596451505753491290)
XLA Ops:
  8.7 3.7 convolution_add_fusion
  29.8 4.2 mul.500
  34.0 5.3 mul.501
  39.3 11.3 %all-gather.5.cloned.1.call-done = bf16[2048,512]{0,1:T(8,128)(2,1)} async-done(((bf16[256,512]{0,1:T(8,128)(2,1)}), bf16[2048,512]{0,1:T(8,128)(2,1)}) %all-gather.5.cloned.1.call-update) | async-done | bytes 2097168 | tf_op jit(solution)/shard_map/all_gather | solution.py:117
  50.6 4.7 copy.200
  55.4 23.2 %all-gather.7.cloned.1.call-done = bf16[2048,512]{1,0:T(8,128)(2,1)} async-done(((bf16[256,512]{1,0:T(8,128)(2,1)}), bf16[2048,512]{1,0:T(8,128)(2,1)}) %all-gather.7.cloned.1.call-update) | async-done | bytes 2097168 | tf_op jit(solution)/shard_map/all_gather | solution.py:118
  78.6 4.0 copy.199
  82.5 4.7 copy.201
  88.0 54.8 %while.30 = (s32[]{:T(128)}, bf16[8,512,64]{1,2,0:T(8,128)(2,1)}, f32[8,512]{1,0:T(8,128)}, bf16[8,512,64]{2,1,0:T(8,128)(2,1)S(1)}, bf16[8,2048,64]{2,1,0:T(8,1...) while((s32[]{:T(128)}, bf16[8,512,64]{1,2,0:T(8,128)(2,1)}, ...), condition=%wide.region_4.5_spmd.clone, body=%wide.region_1.4_spmd.clone.sunk | while | flops 277907968 | bytes 13873273 | solution.py:148
  150.3 8.6 gather_fusion.2
  159.5 9.7 scatter_custom_fusion.1
  169.3 4.5 all-to-all-start.2
  176.8 4.0 reshape.404
  180.8 8.6 scatter_custom_fusion
  189.4 33.3 %all-to-all-done.2 = bf16[8,4,64,1024]{3,2,1,0:T(8,128)(2,1)} async-done(((bf16[8,4,64,1024]{3,2,1,0:T(8,128)(2,1)}), bf16[8,4,64,1024]{3,2,1,0:T(8,128)(2,1)}, u32[]{:S(2)}, u32[]{:S(2)}) %all-to-all-start.2) | async-done | bytes 4194336 | tf_op jit(solution)/shard_map/all_to_all | solution.py:216
  222.6 5.5 all-to-all-start
  228.9 7.8 fusion.52
  236.7 40.3 %all-to-all-done = bf16[8,4,64,1024]{3,2,1,0:T(8,128)(2,1)} async-done(((bf16[8,4,64,1024]{3,2,1,0:T(8,128)(2,1)}), bf16[8,4,64,1024]{3,2,1,0:T(8,128)(2,1)}, u32[]{:S(2)}, u32[]{:S(2)}) %all-to-all-start) | async-done | bytes 4194336 | tf_op jit(solution)/shard_map/all_to_all | solution.py:168
  277.0 7.9 fusion.64
  284.9 12.1 %convert_reduce_fusion.2 = (f32[4,512]{1,0:T(4,128)}, bf16[8,4,64,512]{3,2,0,1:T(8,128)(2,1)}, f32[4,512]{1,0:T(4,128)}, bf16[8,4,64,512]{3,2,0,1:T(8,128)(2,1)}, bf16[8,4,64,512]{3,2,0,1:T(8,128)(2,1)S(1)}) fusion(f32[4,512]{1,0:T(4,128)S(1)} %get-tuple-element.492, f32[4,8,64,512]{3,2,1,0:T(8,128)} %fusion.64, f32[4,512]{1,0:T(4,128)S(1)} %get-tuple-element.493, ...), kind=kOutput, calls=%fused_computation.101 | convolution fusion | flops 2183131136 | bytes 23101440 | tf_op jit(solution)/shard_map/secd,efd->secf/dot_general | solution.py:179
  301.8 5.3 all-to-all-start.1
  307.1 5.3 fusion.63
  312.4 4.7 fusion.46
  319.6 36.5 %all-to-all-done.1 = bf16[8,4,64,1024]{3,2,1,0:T(8,128)(2,1)} async-done(((bf16[8,4,64,1024]{3,2,1,0:T(8,128)(2,1)}), bf16[8,4,64,1024]{3,2,1,0:T(8,128)(2,1)}, u32[]{:S(2)}, u32[]{:S(2)}) %all-to-all-start.1) | async-done | bytes 4194336 | tf_op jit(solution)/shard_map/all_to_all | solution.py:200
  356.0 5.3 all-to-all-start.3
  363.8 8.8 gather_fusion
  372.5 4.8 reshape.373
  377.3 6.5 multiply_reduce_fusion.1
  385.5 24.7 %all-to-all-done.3 = bf16[8,4,64,1024]{3,2,1,0:T(8,128)(2,1)} async-done(((bf16[8,4,64,1024]{3,2,1,0:T(8,128)(2,1)}), bf16[8,4,64,1024]{3,2,1,0:T(8,128)(2,1)}, u32[]{:S(2)}, u32[]{:S(2)}) %all-to-all-start.3) | async-done | bytes 4194336 | tf_op jit(solution)/shard_map/all_to_all | solution.py:269
  410.2 8.8 gather_fusion.1
  419.0 4.7 reshape.374
  425.2 5.7 reduce_sum.188
  433.0 3.2 convert_reduce_fusion.4
  440.5 119.7 %while.31 = (s32[]{:T(128)}, f32[8,512,64]{1,2,0:T(8,128)}, bf16[8,2048,64]{1,2,0:T(8,128)(2,1)}, bf16[8,2048,64]{1,2,0:T(8,128)(2,1)}, f32[8,512]{1,0:T(8,128)S...) while((s32[]{:T(128)}, f32[8,512,64]{1,2,0:T(8,128)}, ...), condition=%wide.region_17.18_spmd.clone, body=%wide.region_15.17_spmd.clone.sunk | while | flops 681739264 | bytes 34763928 | solution.py:328
  554.3 3.1 fusion.160
  560.9 7.2 bitcast_convert_fusion
  568.2 4.1 convert_reduce_fusion
  577.9 12.6 %reduce-scatter.5.cloned.1.call-done = bf16[256,512]{0,1:T(8,128)(2,1)} async-done(((bf16[2048,512]{0,1:T(8,128)(2,1)}), bf16[256,512]{0,1:T(8,128)(2,1)}) %reduce-scatter.5.cloned.1.call-update) | async-done | bytes 262160 | tf_op jit(solution)/shard_map/reduce_scatter | solution.py:334
  591.6 33.7 %reduce-scatter.7.cloned.1.call-done = bf16[256,512]{0,1:T(8,128)(2,1)} async-done(((bf16[2048,512]{0,1:T(8,128)(2,1)}), bf16[256,512]{0,1:T(8,128)(2,1)}) %reduce-scatter.7.cloned.1.call-update) | async-done | bytes 262160 | tf_op jit(solution)/shard_map/reduce_scatter | solution.py:337
  625.3 6.1 fusion.95
  631.8 7.3 fusion.47
  639.1 6.7 fusion.48
  645.8 7.5 pad_maximum_fusion
  656.4 4.9 fusion.94
  661.3 68.9 %all-reduce = (f32[1024]{0:T(1024)}, f32[2048]{0:T(1024)}, f32[1024]{0:T(1024)}, f32[16]{0:T(128)}, f32[1024]{0:T(1024)}, /*index=5*/f32[32]{0:T(128)}) all-reduce(f32[1024]{0:T(1024)S(1)} %get-tuple-element.404, f32[2048]{0:T(1024)S(1)} %convert_reduce_fusion.3, ...), channel_id=1, replica_groups=mesh['dp'=16,'expert'=8] {'dp','expert'}, use_global_device_ids=true, to_apply=%region_22.23 | all-reduce | flops 5168 | bytes 41344 | tf_op jit(solution)/shard_map/psum | solution.py:359
  734.7 151.4 %all-reduce.4.cloned.1.call-done = (f32[1024,2048]{1,0:T(8,128)}, f32[1024,1024]{1,0:T(8,128)}, f32[1024,32]{0,1:T(8,128)}, f32[32,2,512]{2,1,0:T(2,128)}, f32[32,1024]{1,0:T(8,128)}) async-done(((f32[1024,2048]{1,0:T(8,128)}, f32[1024,1024]{1,0:T(8,128)}, f32[1024,32]{0,1:T(8,128)}, f32[32,2,512]{2,1,0:T(2,128)}, f32[32,1024]{1,0:T(8,128)}), (f32[1024,2048]{1,0:T(8,128)}, f32[1024,1024]{1,0:T(8,128)}, ...) | async-done | bytes 12976144 | tf_op jit(solution)/shard_map/psum | solution.py:359
  887.4 83.9 %reduce-scatter.9.cloned.1.call-done = bf16[4,32,2,1024]{3,1,0,2:T(8,128)(2,1)} async-done(((bf16[4,512,2,1024]{3,1,0,2:T(8,128)(2,1)}), bf16[4,32,2,1024]{3,1,0,2:T(8,128)(2,1)}) %reduce-scatter.9.cloned.1.call-update) | async-done | bytes 524304 | tf_op jit(solution)/shard_map/reduce_scatter | solution.py:262
  973.9 8.0 copy.308
  (340 shorter events, 243.4 us)
Async XLA Ops:
  7.2 139.2 %copy-start = (bf16[1024,1024]{1,0:T(8,128)(2,1)S(1)}, bf16[1024,1024]{1,0:T(8,128)(2,1)}, u32[]{:S(2)}) copy-start(bf16[1024,1024]{1,0:T(8,128)(2,1)} %param.28) | copy-start | bytes 6291460
  7.2 43.4 %all-gather.5.cloned.1.call-start = ((), (), s32[]{:S(2)}) async-start(), calls=%async_computation.8 | async-start | bytes 2359296 | tf_op jit(solution)/shard_map/all_gather | solution.py:117
  13.7 10.3 %copy-start.26 = (s32[256,4]{0,1:T(4,128)S(1)}, s32[256,4]{0,1:T(4,128)}, u32[]{:S(2)}) copy-start(s32[256,4]{0,1:T(4,128)} %param.23) | copy-start | bytes 12292
  13.7 10.3 %copy-start.40 = (s32[256,4]{0,1:T(4,128)S(1)}, s32[256,4]{0,1:T(4,128)}, u32[]{:S(2)}) copy-start(s32[256,4]{0,1:T(4,128)} %param.24) | copy-start | bytes 12292
  13.7 10.4 %copy-start.42 = (f32[16]{0:T(128)S(1)}, f32[16]{0:T(128)}, u32[]{:S(2)}) copy-start(f32[16]{0:T(128)} %param.30) | copy-start | bytes 196
  14.5 10.2 %slice-start = ((f32[256,2048]{1,0:T(8,128)}), f32[256,1024]{1,0:T(8,128)S(1)}, s32[]{:S(2)}) async-start(f32[256,2048]{1,0:T(8,128)} %copy-done.10), calls=%async_computation.17 | async-start | bytes 2097152 | tf_op jit(solution)/shard_map/slice | solution.py:110
  17.5 8.6 copy-start.14
  19.4 59.2 %all-gather.7.cloned.1.call-start = ((), (), s32[]{:S(2)}) async-start(), calls=%async_computation.9 | async-start | bytes 2359296 | tf_op jit(solution)/shard_map/all_gather | solution.py:118
  21.2 207.7 %all-gather.11.cloned.1.call-start = ((), (), s32[]{:S(2)}) async-start(), calls=%async_computation.11 | async-start | bytes 4456448 | tf_op jit(solution)/shard_map/all_gather | solution.py:193
  21.9 255.1 %all-gather.9.cloned.1.call-start = ((), (), s32[]{:S(2)}) async-start(), calls=%async_computation.10 | async-start | bytes 8912896 | tf_op jit(solution)/shard_map/all_gather | solution.py:192
  87.9 58.4 %copy-start.30 = (f32[1024]{0:T(1024)S(1)}, f32[1024]{0:T(1024)}, u32[]{:S(2)}) copy-start(f32[1024]{0:T(1024)} %param.29) | copy-start | bytes 12292
  142.8 5.7 copy-start.22
  142.8 6.3 copy-start.28
  142.8 7.2 copy-start.20
  142.8 7.2 copy-start.43
  159.2 10.1 %copy-start.29 = (f32[256]{0:T(256)}, f32[256]{0:T(256)S(1)}, u32[]{:S(2)}) copy-start(f32[256]{0:T(256)S(1)} %get-tuple-element.463) | copy-start | bytes 3076
  159.2 10.0 %copy-start.33 = (f32[256]{0:T(256)}, f32[256]{0:T(256)S(1)}, u32[]{:S(2)}) copy-start(f32[256]{0:T(256)S(1)} %fusion.99) | copy-start | bytes 3076
  169.3 53.4 %all-to-all-start.2 = ((bf16[8,4,64,1024]{3,2,1,0:T(8,128)(2,1)}), bf16[8,4,64,1024]{3,2,1,0:T(8,128)(2,1)}, u32[]{:S(2)}, u32[]{:S(2)}) async-start(bf16[8,4,64,1024]{3,2,1,0:T(8,128)(2,1)} %bitcast.288), calls=%async_computation.2 | async-start | bytes 8388608 | tf_op jit(solution)/shard_map/all_to_all | solution.py:216
  222.6 6.2 copy-start.32
  222.6 54.4 %all-to-all-start = ((bf16[8,4,64,1024]{3,2,1,0:T(8,128)(2,1)}), bf16[8,4,64,1024]{3,2,1,0:T(8,128)(2,1)}, u32[]{:S(2)}, u32[]{:S(2)}) async-start(bf16[8,4,64,1024]{3,2,1,0:T(8,128)(2,1)} %bitcast.289), calls=%async_computation | async-start | bytes 8388608 | tf_op jit(solution)/shard_map/all_to_all | solution.py:168
  277.0 7.9 copy-start.3
  284.9 12.1 %copy-start.44 = (bf16[4,512,1024]{2,1,0:T(8,128)(2,1)S(1)}, bf16[4,512,1024]{2,1,0:T(8,128)(2,1)}, u32[]{:S(2)}) copy-start(bf16[4,512,1024]{2,1,0:T(8,128)(2,1)} %all-gather.11.cloned.1.call-done) | copy-start | bytes 12582916
  301.8 54.2 %all-to-all-start.1 = ((bf16[8,4,64,1024]{3,2,1,0:T(8,128)(2,1)}), bf16[8,4,64,1024]{3,2,1,0:T(8,128)(2,1)}, u32[]{:S(2)}, u32[]{:S(2)}) async-start(bf16[8,4,64,1024]{3,2,1,0:T(8,128)(2,1)} %copy.210), calls=%async_computation.1 | async-start | bytes 8388608 | tf_op jit(solution)/shard_map/all_to_all | solution.py:200
  307.1 5.3 copy-start.12
  356.0 54.2 %all-to-all-start.3 = ((bf16[8,4,64,1024]{3,2,1,0:T(8,128)(2,1)}), bf16[8,4,64,1024]{3,2,1,0:T(8,128)(2,1)}, u32[]{:S(2)}, u32[]{:S(2)}) async-start(bf16[8,4,64,1024]{3,2,1,0:T(8,128)(2,1)} %copy.213), calls=%async_computation.3 | async-start | bytes 8388608 | tf_op jit(solution)/shard_map/all_to_all | solution.py:269
  361.3 229.2 %reduce-scatter.5.cloned.1.call-start = ((), (), s32[]{:S(2)}) async-start(), calls=%async_computation.12 | async-start | bytes 2359296 | tf_op jit(solution)/shard_map/reduce_scatter | solution.py:334
  423.8 7.2 copy-start.35
  425.2 5.7 copy-start.21
  560.3 7.8 copy-start.27
  560.3 65.0 %reduce-scatter.7.cloned.1.call-start = ((), (), s32[]{:S(2)}) async-start(), calls=%async_computation.13 | async-start | bytes 2359296 | tf_op jit(solution)/shard_map/reduce_scatter | solution.py:337
  560.9 172.0 %reduce-scatter.11.cloned.1.call-start = ((), (), s32[]{:S(2)}) async-start(), calls=%async_computation.15 | async-start | bytes 4456448 | tf_op jit(solution)/shard_map/reduce_scatter | solution.py:265
  568.1 4.3 copy-start.39
  568.1 7.1 copy-start.2
  568.1 317.9 %all-reduce.4.cloned.1.call-start = ((), (), s32[]{:S(2)}) async-start(), calls=%async_computation.16 | async-start | bytes 25952256 | tf_op jit(solution)/shard_map/psum | solution.py:359
  568.2 4.3 copy-start.13
  568.2 4.9 copy-start.15
  568.2 4.9 copy-start.18
  568.2 5.9 copy-start.5
  568.2 7.0 copy-start.8
  574.1 17.4 %copy-start.16 = (f32[256,32]{0,1:T(8,128)S(1)}, f32[256,32]{0,1:T(8,128)}, u32[]{:S(2)}) copy-start(f32[256,32]{0,1:T(8,128)} %copy-done.14) | copy-start | bytes 98308
  574.1 17.4 %copy-start.19 = (f32[256,32]{0,1:T(8,128)S(1)}, f32[256,32]{0,1:T(8,128)}, u32[]{:S(2)}) copy-start(f32[256,32]{0,1:T(8,128)} %get-tuple-element.483) | copy-start | bytes 98308
  574.1 51.2 %copy-start.25 = (f32[1024]{0:T(1024)S(1)}, f32[1024]{0:T(1024)}, u32[]{:S(2)}) copy-start(f32[1024]{0:T(1024)} %param.25) | copy-start | bytes 12292
  574.1 51.2 %copy-start.37 = (f32[256]{0:T(256)S(1)}, f32[256]{0:T(256)}, u32[]{:S(2)}) copy-start(f32[256]{0:T(256)} %copy-done.36) | copy-start | bytes 3076
  631.5 339.9 %reduce-scatter.9.cloned.1.call-start = ((), (), s32[]{:S(2)}) async-start(), calls=%async_computation.14 | async-start | bytes 8912896 | tf_op jit(solution)/shard_map/reduce_scatter | solution.py:262
  631.8 7.3 copy-start.11
  656.4 5.0 copy-start.31
  656.4 5.0 copy-start.41
  973.9 8.0 copy-start.9
  (12 other events, 25.1 us)
Sparse Core Ops, SparseCore 0:
  19.5 31.0 all-gather.4
  52.3 26.2 all-gather.6
  80.7 51.4 all-gather.10
  134.8 70.3 all-gather.8
  560.4 30.0 reduce-scatter.4
  592.8 32.5 reduce-scatter.6
  628.6 77.9 reduce-scatter.10
  714.5 171.4 all-reduce.3
  889.5 81.8 reduce-scatter.8
where the time goes:
time: 1010 us; the launch traced here: 992 us
  waiting for transfers between devices  452 us (45%)
  matrix products  216 us (21%)
  local copies, waits for them, and re-layouts  135 us (13%)
  other arithmetic  83.8 us (8%)
  blocking collectives  68.9 us (7%)
  starting transfers between devices  21.3 us (2%)
  between operations  15 us (1%)
    psum x1, waiting for transfers between devices, per_device(): lax.psum((d_attn_gain, d_w_qkv, d_b_qkv, d_w_out, d_b_out, d_sinks, d_moe...  151 us
    reduce_scatter x1, waiting for transfers between devices, per_device(): lax.psum_scatter(gu_term.astype(jnp.bfloat16), 'dp', scatter_dimension=1,...  83.9 us
    psum x1, blocking collectives, per_device(): lax.psum((d_attn_gain, d_w_qkv, d_b_qkv, d_w_out, d_b_out, d_sinks, d_moe...  68.9 us
    all_to_all x1, waiting for transfers between devices, per_device(): lax.all_to_all(send_rows.reshape(groups, exp_local, capacity, model_width...  40.3 us
    dot_general x16, matrix products, head_scores(): jnp.einsum('qd,kd->qk', query_part, key_part, preferred_element_type=jnp....  37.6 us
    all_to_all x1, waiting for transfers between devices, per_device(): lax.all_to_all(expert_out, 'expert', split_axis=0, concat_axis=0, tiled=T...  36.5 us
    reduce_scatter x1, waiting for transfers between devices, per_device(): lax.psum_scatter(value_full.astype(jnp.bfloat16), 'expert', scatter_dimen...  33.7 us
    all_to_all x1, waiting for transfers between devices, per_device(): lax.all_to_all(send_grad.reshape(groups, exp_local, capacity, model_width...  33.3 us
  transfers between devices with their start and end apart: 13, of which 10 were waited for; matrix products, arithmetic and copies ran while one was open for 23% of the time, Pallas kernels for 0%

commit v1 on v0

v1 whole, which is shorter than its diff:
```python
import functools

import jax
import jax.numpy as jnp
import numpy as np
from jax import lax
from jax.experimental import pallas as pl
from jax.experimental.pallas import tpu as pltpu
from jax.sharding import PartitionSpec as P

MESH = pl.DeviceIdType.MESH
BF = jnp.bfloat16
F32 = jnp.float32
EPS = 1e-05
THETA = 10000.0
LIMIT = 7.0
ALPHA = 1.702
NEG = -1000000000.0
NSEM = 800
VLIM = 63 << 20
T = 256
D = 1024


def nt(a, b):
    return lax.dot_general(a, b, (((1,), (1,)), ((), ())), preferred_element_type=F32)


def tn(a, b):
    return lax.dot_general(a, b, (((0,), (0,)), ((), ())), preferred_element_type=F32)


def nn(a, b):
    return jnp.dot(a, b, preferred_element_type=F32)


def split_low(v):
    high = v.astype(BF)
    return high, (v - high.astype(F32)).astype(BF)


def layer_kernel(
    x_in, dy_in, w_in, target, attn_gain, w_qkv, b_qkv, w_out, b_out, sink_row, moe_gain,
    w_rt, b_rt, gu_bias, down_bias, cos_a, sin_a, cos_b, sin_b,
    block_out, d_tokens, d_weights, d_wqkv_t, d_wout, small, d_wrt, d_brt, d_gub,
    xg, dyg, h2g, gathered, qs, kk, vv, kkt, vvt, lse, att_send, att, middle, h2own, metag, meta_send,
    outb, drb, sib_in, half_in, full_in, rs_half, rs_full, rs2_half, rs2_full, dob, dgt_send, dgt_in,
    d_middle, gates_ref, sems, credit,
):
    dp = lax.axis_index("dp")
    g = lax.axis_index("expert")
    y, x = lax.div(dp, 4), lax.rem(dp, 4)
    z, c = lax.div(g, 2), lax.rem(g, 2)
    xs = [lax.rem(x + d, 4) for d in range(4)]
    ys = [lax.rem(y + d, 4) for d in range(4)]
    zs = [lax.rem(z + d, 4) for d in range(4)]
    gs = [lax.rem(g + d, 8) for d in range(8)]
    other = 1 - c
    sib = {"expert": z * 2 + (1 - c)}
    up = {"expert": zs[1] * 2 + c}
    down = {"expert": zs[3] * 2 + c}

    neighbours = {
        "x": [{"dp": y * 4 + xs[d]} for d in range(4)],
        "y": [{"dp": ys[d] * 4 + x} for d in range(4)],
    }

    def xy(axis, d):
        return neighbours[axis][d]

    places = [[[ys[db] * 4 + xs[da] for db in range(4)] for da in range(4)],
              [[ys[da] * 4 + xs[db] for db in range(4)] for da in range(4)]]

    def slot(h, da, db):
        return places[h][da][db]

    counter = [0]

    def sem():
        counter[0] += 1
        assert counter[0] <= NSEM
        return counter[0] - 1

    def sem_block(n):
        first = counter[0]
        counter[0] += n
        assert counter[0] <= NSEM
        return first

    pending = []
    pending_gather = []
    pending_weights = [[] for _ in range(4)]

    def view(ref):
        return ref() if callable(ref) else ref

    def send(src, dst, recv, dev, keep=pending):
        n = sem()

        def copy():
            return pltpu.make_async_remote_copy(
                src_ref=view(src), dst_ref=view(dst), send_sem=sems.at[n], recv_sem=sems.at[recv],
                device_id=dev, device_id_type=MESH)

        copy().start()
        keep.append(copy)

    def arrived(dst, recv):
        pltpu.make_async_remote_copy(
            src_ref=dst, dst_ref=dst, send_sem=sems.at[recv], recv_sem=sems.at[recv],
            device_id=sib, device_id_type=MESH,
        ).wait_recv()

    def drain(copies):
        for copy in copies:
            copy().wait_send()
        copies.clear()

    def local_copy(src, dst):
        n = sem()

        def copy():
            return pltpu.make_async_copy(view(src), view(dst), sems.at[n])

        copy().start()
        return copy

    barrier = pltpu.get_barrier_semaphore()
    for rel in range(1, 8):
        pl.semaphore_signal(barrier, inc=1, device_id={"expert": gs[rel]}, device_id_type=MESH)
    for axis in ("x", "y"):
        for d in (1, 3):
            pl.semaphore_signal(barrier, inc=1, device_id=xy(axis, d), device_id_type=MESH)
    pl.semaphore_wait(barrier, 11)

    class GatherZ:
        def __init__(self, buf, own):
            self.buf, self.own = buf, own
            self.k = sem_block(9)
            self.m1, self.p1, self.far = zs[3] * 2 + c, zs[1] * 2 + c, zs[2] * 2 + c
            s = 1 - c
            self.sm1, self.sp1, self.sfar, self.so = (
                zs[3] * 2 + s, zs[1] * 2 + s, zs[2] * 2 + s, z * 2 + s)

        def start(self):
            b, k = self.buf, self.k
            send(self.own, lambda: b.at[g], k + 1, up, pending_gather)
            send(self.own, lambda: b.at[g], k + 2, down, pending_gather)
            send(self.own, lambda: b.at[g], k + 0, sib, pending_gather)

        def step_m1(self):
            b, k, s = self.buf, self.k, self.m1
            arrived(b.at[s], k + 1)
            send(lambda: b.at[s, pl.ds(0, 128)], lambda: b.at[s, pl.ds(0, 128)], k + 3, up, pending_gather)
            send(lambda: b.at[s], lambda: b.at[s], k + 4, sib, pending_gather)

        def step_p1(self):
            b, k, s = self.buf, self.k, self.p1
            arrived(b.at[s], k + 2)
            send(lambda: b.at[s, pl.ds(128, 128)], lambda: b.at[s, pl.ds(128, 128)], k + 5, down, pending_gather)
            send(lambda: b.at[s], lambda: b.at[s], k + 6, sib, pending_gather)

        def step_far(self):
            b, k, s = self.buf, self.k, self.far
            for i, kr, ks in ((0, 3, 7), (128, 5, 8)):
                arrived(b.at[s, pl.ds(i, 128)], k + kr)
                send(lambda i=i: b.at[s, pl.ds(i, 128)], lambda i=i: b.at[s, pl.ds(i, 128)], k + ks, sib, pending_gather)

        def wait_sib_own(self):
            arrived(self.buf.at[self.so], self.k)

        def wait_sib_m1(self):
            arrived(self.buf.at[self.sm1], self.k + 4)

        def wait_sib_p1(self):
            arrived(self.buf.at[self.sp1], self.k + 6)

        def wait_sib_far(self):
            for i, ks in ((0, 7), (128, 8)):
                arrived(self.buf.at[self.sfar, pl.ds(i, 128)], self.k + ks)

    class ScatterZ:
        def __init__(self, buf, sib_ref, half_ref, full_ref):
            self.buf, self.r, self.h, self.f = buf, sib_ref, half_ref, full_ref
            self.k = sem_block(8)
            self.sent = []

        def chunks(self):
            return [zs[d] * 2 + (1 - c) for d in (2, 1, 3, 0)], [zs[d] * 2 + c for d in (2, 1, 3, 0)]

        def to_sibling(self, n):
            d = (2, 1, 3, 0)[n]
            zz = zs[d]
            send(lambda: self.buf.at[zz * 2 + (1 - c)], lambda: self.r(d), self.k + n, sib, self.sent)

        def add(self, chunk, refs):
            def body(i, carry):
                rows = pl.ds(i * 64, 64)
                v = self.buf[chunk, rows, :].astype(F32)
                for ref in refs:
                    v = v + ref[rows, :].astype(F32)
                self.buf[chunk, rows, :] = v.astype(BF)
                return carry
            lax.fori_loop(0, 4, body, 0)

        def add_half(self, chunk, base, ref):
            def body(i, carry):
                rows = pl.ds(base + i * 64, 64)
                v = self.buf[chunk, rows, :].astype(F32) + ref[pl.ds(i * 64, 64), :].astype(F32)
                self.buf[chunk, rows, :] = v.astype(BF)
                return carry
            lax.fori_loop(0, 2, body, 0)

        def step1(self):
            b, k = self.buf, self.k
            chunk = zs[2] * 2 + c
            arrived(self.r(2), k + 0)
            self.add(chunk, [self.r(2)])
            send(lambda: b.at[chunk, pl.ds(0, 128)], lambda: self.h(0), k + 4, up, self.sent)
            send(lambda: b.at[chunk, pl.ds(128, 128)], lambda: self.h(1), k + 5, down, self.sent)

        def step2(self):
            b, k = self.buf, self.k
            for d, n, hi, dev in ((1, 1, 0, up), (3, 2, 1, down)):
                chunk = zs[d] * 2 + c
                arrived(self.r(d), k + n)
                self.add(chunk, [self.r(d)])
                arrived(self.h(hi), k + 4 + hi)
                self.add_half(chunk, hi * 128, self.h(hi))
                send(lambda chunk=chunk: b.at[chunk], lambda hi=hi: self.f(hi), k + 6 + hi, dev, self.sent)

        def step3(self):
            arrived(self.r(0), self.k + 3)
            arrived(self.f(0), self.k + 6)
            arrived(self.f(1), self.k + 7)

        def result(self, rows):
            return (self.buf[g, rows, :].astype(F32) + self.r(0)[rows, :].astype(F32)
                    + self.f(0)[rows, :].astype(F32) + self.f(1)[rows, :].astype(F32))

    def axis_of(h, ax):
        return "x" if (ax == 0) == (h == 0) else "y"

    gk = sem_block(2 * 4 * 16)

    def gsem(h, e, da, db):
        return gk + ((h * 4 + e) * 4 + da) * 4 + db

    def gsend(h, e, da, db, ax, d):
        def src():
            return w_in.at[h, e] if (da, db) == (0, 0) else gathered.at[h, e, slot(h, da, db)]

        rda, rdb = ((da - d) % 4, db) if ax == 0 else (da, (db - d) % 4)
        send(src, lambda: gathered.at[h, e, slot(h, da, db)], gsem(h, e, rda, rdb), xy(axis_of(h, ax), d % 4),
             pending_weights[e])

    def grecv(h, e, da, db):
        arrived(gathered.at[h, e, slot(h, da, db)], gsem(h, e, da, db))

    def weights_start():
        for e in range(4):
            for h in range(2):
                gsend(h, e, 0, 0, 0, 1)
                gsend(h, e, 0, 0, 0, -1)
            for h in range(2):
                gsend(h, e, 0, 0, 1, 1)
                gsend(h, e, 0, 0, 1, -1)

    def weights_steps():
        for e in range(4):
            for h in range(2):
                grecv(h, e, 3, 0)
                if e % 2 == 0:
                    gsend(h, e, 3, 0, 0, 1)
                grecv(h, e, 1, 0)
                if e % 2 == 1:
                    gsend(h, e, 1, 0, 0, -1)
            for h in range(2):
                for da in (3, 1):
                    gsend(h, e, da, 0, 1, 1)
                    gsend(h, e, da, 0, 1, -1)
            yield "one"
        for e in range(4):
            for h in range(2):
                grecv(h, e, 2, 0)
                gsend(h, e, 2, 0, 1, 1)
                gsend(h, e, 2, 0, 1, -1)
            yield "two"
        for e in range(4):
            for da in (0, 3, 1, 2):
                for h in range(2):
                    grecv(h, e, da, 3)
                    if e % 2 == 0:
                        gsend(h, e, da, 3, 1, 1)
                    grecv(h, e, da, 1)
                    if e % 2 == 1:
                        gsend(h, e, da, 1, 1, -1)
                if da in (3, 2):
                    yield "three"
        for e in range(4):
            for h in range(2):
                for da in range(4):
                    grecv(h, e, da, 2)
            yield ("expert", e)

    small[...] = jnp.zeros((16, D), F32)
    local_x = local_copy(x_in, lambda: xg.at[g])
    gather_x = GatherZ(xg, x_in)
    gather_x.start()
    weights_start()
    local_dy = local_copy(dy_in, lambda: dyg.at[g])
    local_w = []
    for h in range(2):
        for e in range(4):
            local_w.append(local_copy(lambda h=h, e=e: w_in.at[h, e], lambda h=h, e=e: gathered.at[h, e, dp]))
    weights = weights_steps()

    def svc(n=1):
        for _ in range(n):
            if next(weights, None) is None:
                return

    lane = lax.broadcasted_iota(jnp.int32, (1, 128), 1)
    low_half = lane < 64
    first_quarter = (lane % 64) < 32
    mask0 = jnp.where(low_half, 1.0, 0.0).astype(F32)
    mask1 = 1.0 - mask0

    def swap(v):
        return jnp.where(first_quarter, pltpu.roll(v, 96, 1), pltpu.roll(v, 32, 1))

    def trig(r):
        cb, sb = cos_b[pl.ds(r, 1), :], sin_b[pl.ds(r, 1), :]
        ca, sa = cos_a[...], sin_a[...]
        cosine = ca * cb - sa * sb
        sine = sa * cb + ca * sb
        return cosine, jnp.where(first_quarter, -sine, sine)

    def h1_rows(r, rows):
        xf = xg[r, rows, :].astype(F32)
        inv = lax.rsqrt(jnp.mean(xf * xf, axis=-1, keepdims=True) + EPS)
        return (xf * inv * attn_gain[...]).astype(BF)

    def qkv_chunk(r):
        h1 = h1_rows(r, pl.ds(0, T))
        mixed = nn(h1, w_qkv[...]) + b_qkv[...]
        cosine, sine = trig(r)
        q = mixed[:, :128]
        kv = mixed[:, 128:]
        q = (q * cosine + swap(q) * sine) * 0.125
        kv = jnp.where(low_half, kv * cosine + swap(kv) * sine, kv)
        other = pltpu.roll(kv, 64, 1)
        kd = jnp.where(low_half, kv, other)
        vd = jnp.where(low_half, other, kv)
        qs[r] = q.astype(BF)
        kk[r] = kd.astype(BF)
        vv[r] = vd.astype(BF)
        kkt[r] = kd.T.astype(BF)
        vvt[r] = vd.T.astype(BF)

    gx = gather_x
    local_x().wait()
    qkv_chunk(g)
    gx.wait_sib_own()
    qkv_chunk(gx.so)
    gx.step_m1()
    gx.step_p1()
    qkv_chunk(gx.m1)
    svc(1)
    qkv_chunk(gx.p1)
    gx.wait_sib_m1()
    qkv_chunk(gx.sm1)
    svc(1)
    gx.wait_sib_p1()
    qkv_chunk(gx.sp1)
    gx.step_far()
    gather_dy = GatherZ(dyg, dy_in)
    gather_dy.start()
    qkv_chunk(gx.far)
    svc(1)
    gx.wait_sib_far()
    qkv_chunk(gx.sfar)
    svc(1)

    def stacked(v):
        vf = v.astype(F32)
        return jnp.concatenate([vf * mask0, vf * mask1], axis=0).astype(BF)

    key_at = lax.broadcasted_iota(jnp.int32, (T, 2 * T), 0)
    query_at = lax.broadcasted_iota(jnp.int32, (T, 2 * T), 1) % T
    allowed = key_at <= query_at

    att_k = sem_block(8)

    def attend(i, m_ref, l_ref, acc_ref):
        q2 = stacked(qs[i])
        m_ref[...] = sink_row[...]
        l_ref[...] = jnp.ones((1, 2 * T), F32)
        acc_ref[...] = jnp.zeros((128, 2 * T), F32)

        def block(j, diagonal):
            s = nt(kk[j], q2)
            if diagonal:
                s = jnp.where(allowed, s, NEG)
            m_old = m_ref[...]
            m_new = jnp.maximum(m_old, jnp.max(s, axis=0, keepdims=True))
            p = jnp.exp(s - m_new)
            alpha = jnp.exp(m_old - m_new)
            l_ref[...] = l_ref[...] * alpha + jnp.sum(p, axis=0, keepdims=True)
            acc_ref[...] = acc_ref[...] * alpha + nn(vvt[j], p.astype(BF))
            m_ref[...] = m_new

        if i > 0:
            def body(j, carry):
                block(j, False)
                return carry
            lax.fori_loop(0, i, body, 0)
        block(i, True)
        total = l_ref[...]
        lse[i] = m_ref[...] + jnp.log(total)
        o = (acc_ref[...] / total).T
        att_send[i] = jnp.where(low_half, o[:T], o[T:]).astype(BF)

        @pl.when(g != i)
        def _():
            pltpu.make_async_remote_copy(
                src_ref=att_send.at[i], dst_ref=att.at[:, pl.ds(pl.multiple_of(g * 128, 128), 128)],
                send_sem=sems.at[att_sk + i], recv_sem=sems.at[att_k + g],
                device_id={"expert": i}, device_id_type=MESH,
            ).start()

        @pl.when(g == i)
        def _():
            att[:, pl.ds(pl.multiple_of(g * 128, 128), 128)] = att_send[i]

    att_sk = sem_block(8)

    def forward_attention(m_ref, l_ref, acc_ref):
        gd = gather_dy
        for i in range(8):
            attend(i, m_ref, l_ref, acc_ref)
            if i == 3:
                gd.step_m1()
                gd.step_p1()
            if i == 6:
                gd.step_far()
            if i in (1, 2, 4, 5):
                svc(1)

    pl.run_scoped(
        forward_attention, pltpu.VMEM((1, 2 * T), F32), pltpu.VMEM((1, 2 * T), F32), pltpu.VMEM((128, 2 * T), F32))

    for i in range(8):
        @pl.when(g != i)
        def _(i=i):
            piece = att.at[:, pl.ds(i * 128, 128)]
            arrived(piece, att_k + i)
            pltpu.make_async_remote_copy(
                src_ref=att_send.at[i], dst_ref=piece, send_sem=sems.at[att_sk + i],
                recv_sem=sems.at[att_k + i], device_id={"expert": i}, device_id_type=MESH,
            ).wait_send()

    def project(i, carry):
        rows = pl.ds(pl.multiple_of(i * 64, 64), 64)
        m = xg[g, rows, :].astype(F32) + (nn(att[rows, :], w_out[...]) + b_out[...])
        middle[rows, :] = m
        inv = lax.rsqrt(jnp.mean(m * m, axis=-1, keepdims=True) + EPS)
        h2own[rows, :] = (m * inv * moe_gain[...]).astype(BF)
        return carry

    lax.fori_loop(0, 4, project, 0)
    gather_h = GatherZ(h2g, h2own)
    gather_h.start()
    h2g[g] = h2own[...]

    logits = nt(w_rt[...], h2own[...]) + b_rt[...]
    row = lax.broadcasted_iota(jnp.int32, (64, T), 0)
    expert_of_row = jnp.where(row % 8 < 4, (row // 8) * 4 + row % 8, -1)
    slots = jnp.full((64, T), -1.0, F32)
    for k in range(4):
        tgt = target[pl.ds(k, 1), :]
        slots = jnp.where(expert_of_row == tgt // 64, (tgt % 64).astype(F32), slots)
    member = slots >= 0.0
    masked = jnp.where(member, logits, NEG)
    top = jnp.max(masked, axis=0, keepdims=True)
    weight = jnp.where(member, jnp.exp(masked - top), 0.0)
    gates = weight / jnp.sum(weight, axis=0, keepdims=True)
    gates_ref[...] = gates
    for r in range(8):
        meta_send[r, pl.ds(0, 8), :] = gates[r * 8:r * 8 + 8]
        meta_send[r, pl.ds(8, 8), :] = slots[r * 8:r * 8 + 8]
    meta_k = sem_block(8)
    metag[g] = meta_send[g]
    for rel in range(1, 8):
        r = gs[rel]
        send(lambda r=r: meta_send.at[r], lambda: metag.at[g], meta_k + rel, {"expert": r})
    svc(2)
    gh = gather_h
    gh.wait_sib_own()
    gh.step_m1()
    gh.step_p1()
    svc(1)
    gh.step_far()
    for gz in (gather_dy, gh):
        gz.wait_sib_m1()
        gz.wait_sib_p1()
        gz.wait_sib_far()
    gather_dy.wait_sib_own()
    local_dy().wait()
    for rel in range(1, 8):
        arrived(metag.at[gs[8 - rel]], meta_k + rel)
    for copy in local_w:
        copy().wait()

    def weight_of(h, e, n):
        return gathered[h, e, :, pl.ds(n * 16, 16), :].reshape(T, D)

    slot_at = lax.broadcasted_iota(jnp.int32, (64, T), 0).astype(F32)

    def expert(e, rows_ref, grows_ref, dyr_ref, act_ref, dg_ref, du_ref):
        for item in weights:
            if item == ("expert", e):
                break

        def build(s, carry):
            hot = (slot_at == metag[s, pl.ds(8 + e, 1), :]).astype(F32)
            hot_low = hot.astype(BF)
            rows = pl.ds(pl.multiple_of(s * 64, 64), 64)
            rows_ref[rows, :] = nn(hot_low, h2g[s]).astype(BF)
            dyr = nn(hot_low, dyg[s])
            gcol = jnp.sum(hot * metag[s, pl.ds(e, 1), :], axis=1, keepdims=True)
            dyr_ref[rows, :] = dyr.astype(BF)
            grows_ref[rows, :] = (dyr * gcol).astype(BF)
            return carry

        lax.fori_loop(0, 8, build, 0)

        for h in range(2):
            cols = pl.ds(h * T, T)
            bias_g = gu_bias[e, pl.ds(0, 1), cols]
            bias_u = gu_bias[e, pl.ds(1, 1), cols]

            def hidden(i, carry, h=h, cols=cols, bias_g=bias_g, bias_u=bias_u):
                rows = pl.ds(pl.multiple_of(i * 128, 128), 128)
                wg = weight_of(h, e, 0)
                wu = weight_of(h, e, 1)
                wd = weight_of(h, e, 2)
                rv = rows_ref[rows, :]
                gc = LIMIT * jnp.tanh((nt(rv, wg) + bias_g) * (1.0 / LIMIT))
                uc = LIMIT * jnp.tanh((nt(rv, wu) + bias_u) * (1.0 / LIMIT))
                da = nt(grows_ref[rows, :], wd)
                sig = 1.0 / (1.0 + jnp.exp(-ALPHA * gc))
                glu = gc * sig
                act_ref[rows, cols] = ((uc + 1.0) * glu).astype(BF)
                gr, ur = gc * (1.0 / LIMIT), uc * (1.0 / LIMIT)
                dg = da * (uc + 1.0) * (sig + ALPHA * glu * (1.0 - sig)) * (1.0 - gr * gr)
                du = da * glu * (1.0 - ur * ur)
                dg_low, du_low = dg.astype(BF), du.astype(BF)
                dg_ref[rows, cols] = dg_low
                du_ref[rows, cols] = du_low
                return (carry[0] + jnp.sum(dg_low.astype(F32), axis=0, keepdims=True),
                        carry[1] + jnp.sum(du_low.astype(F32), axis=0, keepdims=True))

            zero = jnp.zeros((1, T), F32)
            sum_g, sum_u = lax.fori_loop(0, 4, hidden, (zero, zero))
            d_gub[e, pl.ds(0, 1), cols] = sum_g
            d_gub[e, pl.ds(1, 1), cols] = sum_u

        def outputs(i, carry):
            rows = pl.ds(pl.multiple_of(i * 128, 128), 128)
            out = down_bias[pl.ds(e, 1), :]
            drow = jnp.zeros((128, D), F32)
            for h in range(2):
                cols = pl.ds(h * T, T)
                out = out + nn(act_ref[rows, cols], weight_of(h, e, 2))
                drow = (drow + nn(dg_ref[rows, cols], weight_of(h, e, 0))
                        + nn(du_ref[rows, cols], weight_of(h, e, 1)))
            out_low = out.astype(BF)
            dgate = jnp.sum(dyr_ref[rows, :].astype(F32) * out_low.astype(F32), axis=1, keepdims=True)
            drow_low = drow.astype(BF)
            for n in range(2):
                s = i * 2 + n
                outb[s, pl.ds(e * 64, 64), :] = out_low[n * 64:n * 64 + 64]
                drb[s, pl.ds(e * 64, 64), :] = drow_low[n * 64:n * 64 + 64]
                hot = (slot_at == metag[s, pl.ds(8 + e, 1), :]).astype(F32)
                dgt_send[s, pl.ds(e, 1), :] = jnp.sum(hot * dgate[n * 64:n * 64 + 64], axis=0, keepdims=True)
            return carry + jnp.sum(grows_ref[rows, :].astype(F32), axis=0, keepdims=True)

        small[pl.ds(8 + e, 1), :] = lax.fori_loop(0, 4, outputs, jnp.zeros((1, D), F32))

        drain(pending_weights[e])
        for h in range(2):
            for n, (left, right) in enumerate(((dg_ref, rows_ref), (du_ref, rows_ref), (act_ref, grows_ref))):
                grad = tn(left[:, pl.ds(h * T, T)], right[...])
                gathered[h, e, :, pl.ds(n * 16, 16), :] = grad.astype(BF).reshape(16, 16, D)

    rs_k = sem_block(8 * 9)
    rs_kf = sem_block(8 * 8)
    out_copies = []

    def full_slot(e, h, side, da):
        if e < 2:
            return rs_full.at[e, h, side, da]
        return h2g.at[((e - 2) * 2 + h) * 2 + side, pl.ds(da * 48, 48)]

    def weight_scatter(e, h):
        k = rs_k + (e * 2 + h) * 9
        kf = rs_kf + (e * 2 + h) * 8
        fwd, back = xy(axis_of(h, 1), 1), xy(axis_of(h, 1), 3)
        fwd2, back2 = xy(axis_of(h, 0), 1), xy(axis_of(h, 0), 3)

        def add(s, refs):
            v = gathered[h, e, s].astype(F32)
            for ref in refs:
                v = v + ref[...].astype(F32)
            gathered[h, e, s] = v.astype(BF)

        for n in range(2):
            send(lambda n=n: gathered.at[h, e, slot(h, n, 2)], lambda n=n: rs_half.at[e, h, 0, n], k + n, fwd)
            send(lambda n=n: gathered.at[h, e, slot(h, n + 2, 2)], lambda n=n: rs_half.at[e, h, 1, n], k + 2 + n, back)
        yield 1
        for side, db, dev in ((0, 1, fwd), (1, 3, back)):
            if e == 2:
                pl.semaphore_wait(credit.at[h, side], 1)
            for n in range(2):
                arrived(rs_half.at[e, h, side, n], k + side * 2 + n)
                add(slot(h, side * 2 + n, db), [rs_half.at[e, h, side, n]])
            for da in range(4):
                send(lambda da=da, db=db: gathered.at[h, e, slot(h, da, db)],
                     lambda da=da, side=side: full_slot(e, h, side, da), kf + side * 4 + da, dev)
        yield 2
        for da in (2, 1, 3, 0):
            s = slot(h, da, 0)
            for side in range(2):
                arrived(full_slot(e, h, side, da), kf + side * 4 + da)
            add(s, [full_slot(e, h, 0, da), full_slot(e, h, 1, da)])
            if da == 2:
                send(lambda s=s: gathered.at[h, e, s], lambda: rs2_half.at[e, h], k + 4, fwd2 if e % 2 == 0 else back2)
        yield 3
        arrived(rs2_half.at[e, h], k + 4)
        add(slot(h, 1 if e % 2 == 0 else 3, 0), [rs2_half.at[e, h]])
        send(lambda: gathered.at[h, e, slot(h, 1, 0)], lambda: rs2_full.at[e, h, 0], k + 5, fwd2)
        send(lambda: gathered.at[h, e, slot(h, 3, 0)], lambda: rs2_full.at[e, h, 1], k + 6, back2)
        yield 4
        for side in range(2):
            arrived(rs2_full.at[e, h, side], k + 5 + side)
        add(slot(h, 0, 0), [rs2_full.at[e, h, 0], rs2_full.at[e, h, 1]])
        out_copies.append(local_copy(lambda: gathered.at[h, e, dp], lambda: d_weights.at[h, e]))
        yield 5

    scatters = [[weight_scatter(e, h) for h in range(2)] for e in range(4)]

    def wsvc(*experts):
        for e in experts:
            for h in range(2):
                next(scatters[e][h], None)

    def experts(*refs):
        for e in range(4):
            expert(e, *refs)
            if e == 3:
                drain(pending_gather)
                for h in range(2):
                    pl.semaphore_signal(credit.at[h, 1], inc=1, device_id=xy(axis_of(h, 1), 1), device_id_type=MESH)
                    pl.semaphore_signal(credit.at[h, 0], inc=1, device_id=xy(axis_of(h, 1), 3), device_id_type=MESH)
            wsvc(e)
            if e >= 1:
                wsvc(e - 1)

    pl.run_scoped(
        experts,
        pltpu.VMEM((512, D), BF), pltpu.VMEM((512, D), BF), pltpu.VMEM((512, D), BF),
        pltpu.VMEM((512, 512), BF), pltpu.VMEM((512, 512), BF), pltpu.VMEM((512, 512), BF))

    dg_k = sem_block(8)
    dgt_in[g] = dgt_send[g]
    for rel in range(1, 8):
        r = gs[rel]
        send(lambda r=r: dgt_send.at[r], lambda: dgt_in.at[g], dg_k + rel, {"expert": r})

    def combine(buf, s, gated):
        pieces = []
        for e in range(4):
            hot = (slot_at == metag[s, pl.ds(8 + e, 1), :]).astype(F32)
            if gated:
                hot = hot * metag[s, pl.ds(e, 1), :]
            pieces.append(hot)
        spread = jnp.concatenate(pieces, axis=0).T.astype(BF)
        buf[s] = nn(spread, buf[s]).astype(BF)

    scatter_d = ScatterZ(drb, lambda n: sib_in.at[n], lambda n: half_in.at[n], lambda n: full_in.at[n])
    far_chunks, own_chunks = scatter_d.chunks()
    for n in range(4):
        combine(drb, far_chunks[n], False)
        scatter_d.to_sibling(n)
    combine(drb, own_chunks[0], False)
    scatter_d.step1()
    combine(drb, own_chunks[1], False)
    combine(drb, own_chunks[2], False)
    wsvc(0)
    scatter_d.step2()
    combine(drb, own_chunks[3], False)
    wsvc(3)
    for n in range(4):
        combine(outb, far_chunks[n], True)
    for n in range(4):
        combine(outb, own_chunks[n], True)
    wsvc(0)
    scatter_d.step3()

    for rel in range(1, 8):
        arrived(dgt_in.at[gs[8 - rel]], dg_k + rel)
    d_gates = jnp.where(row % 8 < 4, jnp.concatenate([dgt_in[r] for r in range(8)], axis=0), 0.0)
    d_logits = gates_ref[...] * (d_gates - jnp.sum(gates_ref[...] * d_gates, axis=0, keepdims=True))
    dl_high, dl_low = split_low(d_logits)
    d_wrt[...] = nn(dl_high, h2own[...]) + nn(dl_low, h2own[...])
    d_brt[...] = jnp.broadcast_to(jnp.sum(d_logits, axis=1, keepdims=True), (64, 128))
    dl_high_t, dl_low_t = split_low(d_logits.T)
    d_middle[...] = nn(dl_high_t, w_rt[...]) + nn(dl_low_t, w_rt[...])
    drain(scatter_d.sent)
    att_at, branch_at = gs[1], gs[2]

    def middle_back(i, carry):
        rows = pl.ds(pl.multiple_of(i * 64, 64), 64)
        m = middle[rows, :]
        inv = lax.rsqrt(jnp.mean(m * m, axis=-1, keepdims=True) + EPS)
        d_h2 = scatter_d.result(rows) + d_middle[rows, :]
        v2 = d_h2 * moe_gain[...]
        inner = jnp.mean(v2 * m, axis=-1, keepdims=True)
        dm = dyg[g, rows, :].astype(F32) + inv * v2 - m * (inv * inv * inv * inner)
        d_middle[rows, :] = dm
        low = dm.astype(BF)
        drb[branch_at, rows, :] = low
        drb[att_at, rows, :] = nt(low, w_out[...]).astype(BF)
        return (carry[0] + jnp.sum(low.astype(F32), axis=0, keepdims=True),
                carry[1] + jnp.sum(d_h2 * m * inv, axis=0, keepdims=True))

    zero_row = jnp.zeros((1, D), F32)
    sum_b, sum_m = lax.fori_loop(0, 4, middle_back, (zero_row, zero_row))
    small[pl.ds(1, 1), :] = sum_b
    small[pl.ds(2, 1), :] = sum_m

    do_k = sem_block(8)
    att_sent = []
    dob[g] = drb[att_at, :, pl.ds(pl.multiple_of(g * 128, 128), 128)]
    for rel in range(1, 8):
        r = gs[rel]
        send(lambda r=r: drb.at[att_at, :, pl.ds(pl.multiple_of(r * 128, 128), 128)], lambda: dob.at[g], do_k + rel, {"expert": r}, att_sent)

    def wout_part(stage_ref):
        for n in range(4):
            rows = pl.ds(n * 256, 256)
            stage_ref[rows, :] = tn(att[:, rows], drb[branch_at]).astype(BF)
        wsvc(1)
        local_copy(stage_ref, d_wout)().wait()

    pl.run_scoped(wout_part, pltpu.VMEM((D, D), BF))
    for rel in range(1, 8):
        arrived(dob.at[gs[8 - rel]], do_k + rel)

    scatter_m = ScatterZ(
        outb, lambda n: dyg.at[n], lambda n: dyg.at[4, pl.ds(n * 128, 128)], lambda n: dyg.at[5 + n])
    for n in range(4):
        scatter_m.to_sibling(n)

    sub_low = lax.broadcasted_iota(jnp.int32, (128, 1), 0) < 64
    smask0 = jnp.where(sub_low, 1.0, 0.0).astype(F32)
    smask1 = 1.0 - smask0

    def stacked_t(v_t):
        return jnp.concatenate([v_t * smask0, v_t * smask1], axis=1).astype(BF)

    def attend_back(i, dk_ref, dv_ref, dqkv_ref, dq_ref):
        q2 = stacked(qs[i])
        q2t = stacked_t(qs[i].astype(F32).T)
        do2 = stacked(dob[i])
        do_t = dob[i].astype(F32).T
        do2t = stacked_t(do_t)
        prod = do_t * att_send[i].astype(F32).T
        delta = jnp.concatenate(
            [jnp.sum(prod[:64], axis=0, keepdims=True), jnp.sum(prod[64:], axis=0, keepdims=True)], axis=1)
        lse_row = lse[i]
        small[pl.ds(4, 1), pl.ds(0, 512)] -= jnp.exp(sink_row[...] - lse_row) * delta
        dq_ref[...] = jnp.zeros((128, 2 * T), F32)

        def block(j, diagonal):
            p = jnp.exp(nn(kk[j], q2t) - lse_row)
            if diagonal:
                p = jnp.where(allowed, p, 0.0)
            ds = (p * (nn(vv[j], do2t) - delta)).astype(BF)
            dv_ref[j] += nn(p.astype(BF), do2)
            dk_ref[j] += nn(ds, q2)
            dq_ref[...] += nn(kkt[j], ds)

        if i > 0:
            def body(j, carry):
                block(j, False)
                return carry
            lax.fori_loop(0, i, body, 0)
        block(i, True)
        dq = dq_ref[...].T
        dq = jnp.where(low_half, dq[:T], dq[T:]) * 0.125
        cosine, sine = trig(i)
        dqkv_ref[i, :, pl.ds(0, 128)] = (dq * cosine - swap(dq) * sine).astype(BF)

    def backward(dk_ref, dv_ref, dqkv_ref, dq_ref, dw_ref):
        dk_ref[...] = jnp.zeros((8, T, 128), F32)
        dv_ref[...] = jnp.zeros((8, T, 128), F32)
        plan = {0: (1,), 1: (0,), 2: (2,), 3: (1,), 4: (3,), 5: (2,), 6: (3,), 7: (2,)}
        for i in range(8):
            attend_back(i, dk_ref, dv_ref, dqkv_ref, dq_ref)
            wsvc(*plan[i])
            if i == 3:
                scatter_m.step1()
            if i == 5:
                scatter_m.step2()
        drain(att_sent)

        def finish(r, carry):
            cosine, sine = trig(r)
            dk = dk_ref[r]
            dk = dk + pltpu.roll(dk, 64, 1)
            dv = dv_ref[r]
            dv = dv + pltpu.roll(dv, 64, 1)
            dkv = jnp.where(low_half, dk * cosine - swap(dk) * sine, dv)
            dqkv_ref[r, :, pl.ds(128, 128)] = dkv.astype(BF)
            return carry + jnp.sum(dqkv_ref[r].astype(F32), axis=0, keepdims=True)

        small[pl.ds(3, 1), pl.ds(0, T)] = lax.fori_loop(0, 8, finish, jnp.zeros((1, T), F32))

        scatter_h = ScatterZ(drb, lambda n: sib_in.at[n], lambda n: half_in.at[n], lambda n: full_in.at[n])

        def d_h1_chunk(s):
            drb[s] = nt(dqkv_ref[s], w_qkv[...]).astype(BF)

        for n in range(4):
            d_h1_chunk(far_chunks[n])
            scatter_h.to_sibling(n)
        d_h1_chunk(own_chunks[0])
        scatter_h.step1()
        d_h1_chunk(own_chunks[1])
        d_h1_chunk(own_chunks[2])
        scatter_h.step2()
        d_h1_chunk(own_chunks[3])

        dw_ref[...] = jnp.zeros((T, D), F32)

        def dw_part(r, carry):
            dw_ref[...] += tn(dqkv_ref[r], h1_rows(r, pl.ds(0, T)))
            return carry

        lax.fori_loop(0, 8, dw_part, 0)
        cp = local_copy(dw_ref, d_wqkv_t)
        scatter_m.step3()

        def result(i, carry):
            rows = pl.ds(pl.multiple_of(i * 64, 64), 64)
            att[rows, :] = (middle[rows, :] + scatter_m.result(rows)).astype(BF)
            return carry

        lax.fori_loop(0, 4, result, 0)
        cp2 = local_copy(att, block_out)
        wsvc(3)
        scatter_h.step3()

        def tokens_back(i, carry):
            rows = pl.ds(pl.multiple_of(i * 64, 64), 64)
            xf = xg[g, rows, :].astype(F32)
            inv = lax.rsqrt(jnp.mean(xf * xf, axis=-1, keepdims=True) + EPS)
            d_h1 = scatter_h.result(rows)
            v1 = d_h1 * attn_gain[...]
            inner = jnp.mean(v1 * xf, axis=-1, keepdims=True)
            h2own[rows, :] = (d_middle[rows, :] + inv * v1 - xf * (inv * inv * inv * inner)).astype(BF)
            return carry + jnp.sum(d_h1 * xf * inv, axis=0, keepdims=True)

        small[pl.ds(0, 1), :] = lax.fori_loop(0, 4, tokens_back, zero_row)
        cp3 = local_copy(h2own, d_tokens)
        wsvc(3)
        drain(scatter_h.sent)
        drain(scatter_m.sent)
        for copy in (cp, cp2, cp3):
            copy().wait()

    pl.run_scoped(
        backward, pltpu.VMEM((8, T, 128), F32), pltpu.VMEM((8, T, 128), F32), pltpu.VMEM((8, T, T), BF),
        pltpu.VMEM((128, 2 * T), F32), pltpu.VMEM((T, D), F32))
    for e in range(4):
        wsvc(e, e, e, e)
    drain(pending)
    for copy in out_copies:
        copy().wait()


ANY = pl.BlockSpec(memory_space=pl.ANY)
VM = pl.BlockSpec(memory_space=pltpu.VMEM)


def angle_tables():
    frequency = np.exp(np.arange(32, dtype=np.float32) * np.float32(-2.0 * np.log(THETA) / 64)).astype(np.float64)
    freq = np.tile(frequency, 4)[None, :]
    near = np.arange(T, dtype=np.float64)[:, None] * freq
    far = np.arange(8, dtype=np.float64)[:, None] * T * freq
    return [f(a).astype(np.float32) for a in (near, far) for f in (np.cos, np.sin)]


def per_device(
    tokens, cotangent, routes, slot_ids, attn_gain, w_qkv, b_qkv, w_out, b_out, sink_logits, moe_gain,
    w_router, b_router, gu_weight, gu_bias, down_weight, down_bias,
):
    g = lax.axis_index("expert")
    both = jnp.concatenate([gu_weight.transpose(0, 2, 1, 3), down_weight[:, None]], axis=1)
    shard = both.reshape(4, 3, 2, 16, D).transpose(2, 0, 1, 3, 4).reshape(2, 4, 48, D)
    target = jnp.pad((routes * 64 + slot_ids).T, ((0, 4), (0, 0)))

    def own_columns(v):
        return jnp.concatenate(
            [lax.dynamic_slice_in_dim(v, g * 128, 128, 1), lax.dynamic_slice_in_dim(v, 1024 + g * 64, 64, 1),
             lax.dynamic_slice_in_dim(v, 1536 + g * 64, 64, 1)], axis=1)

    sinks = jnp.repeat(lax.dynamic_slice_in_dim(sink_logits, g * 2, 2, 0), T)[None, :]

    def padded(v):
        return jnp.pad(v.reshape(8, 4, -1), ((0, 0), (0, 4), (0, 0))).reshape(64, -1)

    w_rt = padded(w_router.T)
    b_rt = jnp.broadcast_to(padded(b_router), (64, T))
    gub = gu_bias.reshape(4, 2, 16, 2, 16).transpose(0, 1, 3, 2, 4).reshape(4, 2, 512)
    down_own = lax.dynamic_slice_in_dim(down_bias, g * 4, 4, 0)
    cos_a, sin_a, cos_b, sin_b = [jnp.asarray(t) for t in angle_tables()]
    shape = jax.ShapeDtypeStruct
    out = pl.pallas_call(
        layer_kernel,
        out_shape=(
            shape((T, D), BF), shape((T, D), BF), shape((2, 4, 48, D), BF), shape((T, D), F32), shape((D, D), BF),
            shape((16, D), F32), shape((64, D), F32), shape((64, 128), F32), shape((4, 2, 512), F32),
        ),
        in_specs=[ANY, ANY, ANY] + [VM] * 16,
        out_specs=[ANY, ANY, ANY, ANY, ANY, VM, VM, VM, VM],
        scratch_shapes=[
            pltpu.VMEM((8, T, D), BF), pltpu.VMEM((8, T, D), BF), pltpu.VMEM((8, T, D), BF),
            pltpu.VMEM((2, 4, 16, 48, D), BF),
            pltpu.VMEM((8, T, 128), BF), pltpu.VMEM((8, T, 128), BF), pltpu.VMEM((8, T, 128), BF),
            pltpu.VMEM((8, 128, T), BF), pltpu.VMEM((8, 128, T), BF),
            pltpu.VMEM((8, 1, 2 * T), F32), pltpu.VMEM((8, T, 128), BF), pltpu.VMEM((T, D), BF),
            pltpu.VMEM((T, D), F32), pltpu.VMEM((T, D), BF),
            pltpu.VMEM((8, 16, T), F32), pltpu.VMEM((8, 16, T), F32),
            pltpu.VMEM((8, T, D), BF), pltpu.VMEM((8, T, D), BF),
            pltpu.VMEM((4, T, D), BF), pltpu.VMEM((2, 128, D), BF), pltpu.VMEM((2, T, D), BF),
            pltpu.VMEM((4, 2, 2, 2, 48, D), BF), pltpu.VMEM((2, 2, 2, 4, 48, D), BF),
            pltpu.VMEM((4, 2, 48, D), BF), pltpu.VMEM((4, 2, 2, 48, D), BF),
            pltpu.VMEM((8, T, 128), BF), pltpu.VMEM((8, 8, T), F32), pltpu.VMEM((8, 8, T), F32),
            pltpu.VMEM((T, D), F32),
            pltpu.VMEM((64, T), F32),
            pltpu.SemaphoreType.DMA((NSEM,)), pltpu.SemaphoreType.REGULAR((2, 2)),
        ],
        compiler_params=pltpu.CompilerParams(collective_id=1, has_side_effects=True, vmem_limit_bytes=VLIM),
    )(tokens, cotangent, shard, target, attn_gain[None], own_columns(w_qkv), own_columns(b_qkv[None]), w_out, b_out[None],
      sinks, moe_gain[None], w_rt, b_rt, gub, down_own, cos_a, sin_a, cos_b, sin_b)
    block_out, d_tokens, d_weights, d_wq, d_wo, small, d_wrt, d_brt, d_gub = out

    def unpadded(v):
        return v.reshape(8, 8, -1)[:, :4].reshape(32, -1)

    d_wq = lax.all_gather(lax.psum(d_wq, "dp"), "expert", axis=0)
    own = lax.all_gather(lax.psum((small[3, :256], small[4, :512].reshape(2, 256).sum(1), small[8:12]), "dp"), "expert", axis=0)
    d_bq, d_sinks, d_down_bias = own
    every = lax.psum((small[0], small[1], small[2], unpadded(d_wrt), unpadded(d_brt)[:, 0], d_wo.astype(F32)), ("dp", "expert"))

    def whole(v):
        return jnp.concatenate([v[:, :128].reshape((1024,) + v.shape[2:]), v[:, 128:192].reshape((512,) + v.shape[2:]),
                                v[:, 192:].reshape((512,) + v.shape[2:])], axis=0)

    d_gub = lax.psum_scatter(d_gub.reshape(4, 2, 2, 16, 16).transpose(3, 0, 1, 2, 4).reshape(16, 4, 2, 32), "dp", scatter_dimension=0, tiled=False)
    dw = d_weights.astype(F32).reshape(2, 4, 3, 16, D).transpose(1, 0, 3, 2, 4).reshape(4, 32, 3, D)
    return (
        block_out, d_tokens, every[0], whole(d_wq).T, whole(d_bq), every[5], every[1], d_sinks.reshape(16),
        every[2], every[3].T, every[4], dw[:, :, :2], d_gub, dw[:, :, 2], d_down_bias.reshape(32, D),
    )


def solution(mesh):
    rows = P(("dp", "expert"), None)
    in_specs = (rows,) * 4 + (P(),) * 9 + (
        P("expert", "dp", None, None), P("expert", None, None), P("expert", "dp", None), P())
    out_specs = (rows,) * 2 + (P(),) * 9 + (
        P("expert", "dp", None, None), P("expert", None, "dp"), P("expert", "dp", None), P())
    return jax.shard_map(per_device, mesh=mesh, in_specs=in_specs, out_specs=out_specs, check_vma=False)
```

time: 1010 us -> 608 us (0.60)
  waiting for transfers between devices: 452 us -> 85.8 us
  Pallas kernels: 0 us -> 233 us
  matrix products: 216 us -> 0 us
  blocking collectives: 68.9 us -> 211 us
  local copies, waits for them, and re-layouts: 135 us -> 42.4 us
  other arithmetic: 83.8 us -> 10.3 us
  starting transfers between devices: 21.3 us -> 0.38 us
    pallas_call x0 -> x1, Pallas kernels: none -> 233 us  [per_device(): pl.pallas_call(layer_kernel, out_shape=(shape((T, D), BF), shape((T, D),...]
    dot_general x74 -> x0, matrix products: 216 us -> none  [the longest x16 37.6 us: head_scores(): jnp.einsum('qd,kd->qk', query_part, key_part, preferred_element_type=jnp....]
    all_to_all x4 -> x0, waiting for transfers between devices: 135 us -> none  [the longest x1 40.3 us: per_device(): lax.all_to_all(send_rows.reshape(groups, exp_local, capacity, model_width...]
    reduce_scatter x4 -> x0, waiting for transfers between devices: 130 us -> none  [the longest x1 83.9 us: per_device(): lax.psum_scatter(gu_term.astype(jnp.bfloat16), 'dp', scatter_dimension=1,...]
    psum x1 -> x2, blocking collectives: 68.9 us -> 163 us  [the longest x1 104 us: per_device(): lax.psum((small[0], small[1], small[2], unpadded(d_wrt), unpadded(d_brt)[...]
    psum x1 -> x2, waiting for transfers between devices: 151 us -> 85.8 us  [the longest x1 85.8 us: per_device(): d_wq = lax.all_gather(lax.psum(d_wq, 'dp'), 'expert', axis=0)]
    all_gather x0 -> x3, blocking collectives: none -> 47.3 us  [per_device(): lax.all_gather(lax.psum((small[3, :256], small[4, :512].reshape(2, 256).s...]
    all_gather x4 -> x1, waiting for transfers between devices: 34.5 us -> 0.01 us  [per_device(): d_wq = lax.all_gather(lax.psum(d_wq, 'dp'), 'expert', axis=0)]
  transfers between devices with their start and end apart: 13 -> 3, of which waited for: 10 -> 1; matrix products, arithmetic and copies ran while one was open for 23% -> 6% of each run, Pallas kernels for 0% -> 0%
where the time goes in v1:
time: 608 us; the launch traced here: 598 us
  Pallas kernels  233 us (38%)
  blocking collectives  211 us (35%)
  waiting for transfers between devices  85.8 us (14%)
  local copies, waits for them, and re-layouts  42.4 us (7%)
  between operations  16.2 us (3%)
  other arithmetic  10.3 us (2%)
    pallas_call x1, Pallas kernels, per_device(): pl.pallas_call(layer_kernel, out_shape=(shape((T, D), BF), shape((T, D),...  233 us
    psum x1, blocking collectives, per_device(): lax.psum((small[0], small[1], small[2], unpadded(d_wrt), unpadded(d_brt)[...  104 us
    psum x1, waiting for transfers between devices, per_device(): d_wq = lax.all_gather(lax.psum(d_wq, 'dp'), 'expert', axis=0)  85.8 us
    psum x1, blocking collectives, per_device(): lax.psum((small[3, :256], small[4, :512].reshape(2, 256).sum(1), small[8:...  59.2 us
    all_gather x3, blocking collectives, per_device(): lax.all_gather(lax.psum((small[3, :256], small[4, :512].reshape(2, 256).s...  47.3 us
  transfers between devices with their start and end apart: 3, of which 1 were waited for; matrix products, arithmetic and copies ran while one was open for 6% of the time, Pallas kernels for 0%

profile of v1, /device:TPU:1, one launch (start us, length us, event | category | flops | bytes accessed | tf_op | source)
XLA Modules:
  0.0 598.5 jit_solution(16053807397188947914)
XLA Ops:
  8.1 1.1 constant_dynamic-slice_fusion.3
  9.2 1.3 constant_dynamic-slice_fusion.2
  10.5 0.8 dynamic-slice_bitcast_fusion.2
  11.3 0.8 dynamic-slice_bitcast_fusion.3
  12.1 0.7 dynamic_slice.30
  12.9 0.6 copy.75
  13.5 1.2 copy.64
  14.6 0.2 reshape.113
  14.9 0.7 reshape.114.gu_bias
  15.6 0.7 pad_bitcast_fusion.w_rt
  16.5 0.6 pad.12.target
  17.1 0.6 constant_dynamic-slice_fusion.down_bias
  17.7 0.9 pad_maximum_fusion
  18.7 1.0 pad_maximum_fusion.1.w_qkv
  19.6 0.6 pad_maximum_fusion.3.b_qkv
  20.3 0.7 broadcast_in_dim.26.b_rt
  21.0 232.8 %shard_map.316 = (bf16[256,1024]{1,0:T(8,128)(2,1)}, bf16[256,1024]{1,0:T(8,128)(2,1)}, bf16[2,4,48,1024]{3,2,1,0:T(8,128)(2,1)}, f32[256,1024]{1,0:T(8,128)}, b...) custom-call(bf16[256,1024]{1,0:T(8,128)(2,1)} %x_in.1, ...), custom_call_target="tpu_custom_call" | custom-call | tf_op jit(solution)/shard_map/pallas_call | solution.py:931
  253.9 85.8 %all-reduce.10.cloned.1.call-done = f32[1,256,1024]{2,1,0:T(8,128)} async-done(((f32[1,256,1024]{2,1,0:T(8,128)}), f32[1,256,1024]{2,1,0:T(8,128)}) %all-reduce.10.cloned.1.call-update) | async-done | bytes 1048592 | tf_op jit(solution)/shard_map/psum | solution.py:964
  339.7 0.3 all-reduce.12.cloned.1.call-start
  340.0 0.7 reshape.123
  340.7 0.8 slice_bitcast_fusion.1
  341.5 0.7 slice_reduce_fusion.1
  342.2 0.7 slice.55
  343.4 59.2 %all-reduce.5 = (f32[1,256]{1,0:T(1,128)S(1)}, f32[1,2]{1,0:T(1,128)S(1)}, f32[16,4,2,32]{3,1,2,0:T(4,128)S(1)}, f32[1,4,1024]{2,1,0:T(4,128)S(1)}) all-reduce(f32[1,256]{1,0:T(1,128)S(1)} %slice.55, f32[1,2]{1,0:T(1,128)S(1)} %bitcast.94, f32[16,4,2,32]{3,1,2,0:T(4,128)S(1)} %reshape.130, ...), channel_id=1, replica_groups=mesh['dp'=16,'expert'=8] {'dp'}, use_global_device_ids=true, to_apply=%region_2.3 | all-reduce | flops 8450 | bytes 67600 | tf_op jit(solution)/shard_map/psum | solution.py:965
  402.6 26.5 %all-gather = f32[8,1,256]{2,1,0:T(1,128)S(1)} all-gather(f32[1,1,256]{2,1,0:T(1,128)S(1)} %bitcast.95), channel_id=1, replica_groups=mesh['dp'=16,'expert'=8] {'expert'}, dimensions={0}, use_global_device_ids=true | all-gather | bytes 9216 | tf_op jit(solution)/shard_map/all_gather | solution.py:965
  429.2 0.9 fusion.1
  430.6 0.8 slice_bitcast_fusion
  431.6 12.8 %all_gather.31 = f32[8,4,1024]{2,1,0:T(4,128)S(1)} all-gather(f32[1,4,1024]{2,1,0:T(4,128)S(1)} %get-tuple-element.101), channel_id=1, replica_groups=mesh['dp'=16,'expert'=8] {'expert'}, dimensions={0}, use_global_device_ids=true | all-gather | bytes 147456 | tf_op jit(solution)/shard_map/all_gather | solution.py:965
  444.4 0.7 reshape.131
  445.1 0.6 dynamic-slice.12
  445.7 0.6 dynamic-slice_bitcast_fusion
  446.3 0.6 copy.73
  446.9 8.0 %all-gather.1 = f32[8,1,2]{2,1,0:T(1,128)S(1)} all-gather(f32[1,1,2]{2,1,0:T(1,128)S(1)} %bitcast.96), channel_id=1, replica_groups=mesh['dp'=16,'expert'=8] {'expert'}, dimensions={0}, use_global_device_ids=true | all-gather | bytes 72 | tf_op jit(solution)/shard_map/all_gather | solution.py:965
  454.9 0.5 broadcast.13
  455.5 0.7 reduce.9
  456.1 0.6 reshape.121
  456.8 1.8 copy.72
  458.6 0.6 pad_maximum_fusion.2
  459.2 104.0 %all-reduce.13 = (f32[1024]{0:T(1024)}, f32[1024,1024]{1,0:T(8,128)}, f32[1024]{0:T(1024)}, f32[1024]{0:T(1024)}, f32[32]{0:T(128)}) all-reduce(f32[1024]{0:T(1024)S(1)} %bitcast.88, bf16[1024,1024]{1,0:T(8,128)(2,1)S(1)} %copy-done.1, f32[1024]{0:T(1024)S(1)} %bitcast.87, ...), channel_id=1, replica_groups=mesh['dp'=16,'expert'=8] {'dp','expert'}, use_global_device_ids=true, to_apply=%region_0.1 | all-reduce | flops 1051680 | bytes 6316288 | tf_op jit(solution)/shard_map/psum | solution.py:967
  563.2 4.8 slice.68
  568.0 5.4 copy.67
  573.4 4.0 fusion
  577.4 2.9 copy.68
  580.3 1.9 copy.69
  582.2 6.2 %maximum_bitcast_fusion = f32[1024,2048]{1,0:T(8,128)} fusion(f32[512,1024]{0,1:T(8,128)} %copy.69, f32[512,1024]{0,1:T(8,128)} %copy.68, f32[1024,1024]{0,1:T(8,128)} %copy.67), kind=kLoop, calls=%fused_computation | loop fusion | flops 4194304 | bytes 16777216 | tf_op jit(solution)/shard_map/transpose | solution.py:976
  588.3 0.8 copy.92
  589.1 0.8 copy.93
  589.9 0.7 copy.94
  (62 shorter events, 1.8 us)
Async XLA Ops:
  8.0 9.1 %copy-start = (f32[32,1024]{1,0:T(8,128)S(1)}, f32[32,1024]{1,0:T(8,128)}, u32[]{:S(2)}) copy-start(f32[32,1024]{1,0:T(8,128)} %param.37) | copy-start | bytes 393220
  8.0 6.6 %copy-start.9 = (f32[4,2,512]{2,1,0:T(2,128)S(1)}, f32[4,2,512]{2,1,0:T(2,128)}, u32[]{:S(2)}) copy-start(f32[4,2,512]{2,1,0:T(2,128)} %param.35) | copy-start | bytes 49156
  8.0 7.6 %copy-start.8 = (bf16[1024,32]{0,1:T(8,128)(2,1)S(1)}, bf16[1024,32]{0,1:T(8,128)(2,1)}, u32[]{:S(2)}) copy-start(bf16[1024,32]{0,1:T(8,128)(2,1)} %param.32) | copy-start | bytes 196612
  8.1 8.3 %copy-start.14 = (f32[32]{0:T(128)S(1)}, f32[32]{0:T(128)}, u32[]{:S(2)}) copy-start(f32[32]{0:T(128)} %param.33) | copy-start | bytes 388
  8.1 8.4 %copy-start.13 = (s32[256,4]{0,1:T(4,128)S(1)}, s32[256,4]{0,1:T(4,128)}, u32[]{:S(2)}) copy-start(s32[256,4]{0,1:T(4,128)} %param.23) | copy-start | bytes 12292
  8.1 8.4 %copy-start.12 = (s32[256,4]{0,1:T(4,128)S(1)}, s32[256,4]{0,1:T(4,128)}, u32[]{:S(2)}) copy-start(s32[256,4]{0,1:T(4,128)} %param.24) | copy-start | bytes 12292
  8.1 9.7 %copy-start.5 = (bf16[4,32,1024]{2,1,0:T(8,128)(2,1)S(1)}, bf16[4,32,1024]{2,1,0:T(8,128)(2,1)}, u32[]{:S(2)}) copy-start(bf16[4,32,1024]{2,1,0:T(8,128)(2,1)} %param.36) | copy-start | bytes 786436
  8.1 331.6 %all-reduce.10.cloned.1.call-start = ((), (), s32[]{:S(2)}) async-start(), calls=%async_computation | async-start | bytes 2097152 | tf_op jit(solution)/shard_map/psum | solution.py:964
  253.8 86.2 %copy-start.7 = (f32[64,1024]{1,0:T(8,128)S(1)}, f32[64,1024]{1,0:T(8,128)}, u32[]{:S(2)}) copy-start(f32[64,1024]{1,0:T(8,128)} %get-tuple-element.29) | copy-start | bytes 786436
  253.8 89.1 %copy-start.10 = (f32[4,2,512]{2,1,0:T(2,128)S(1)}, f32[4,2,512]{2,1,0:T(2,128)}, u32[]{:S(2)}) copy-start(f32[4,2,512]{2,1,0:T(2,128)} %get-tuple-element.32) | copy-start | bytes 49156
  253.8 176.3 %copy-start.2 = (bf16[2,4,48,1024]{3,2,1,0:T(8,128)(2,1)S(1)}, bf16[2,4,48,1024]{3,2,1,0:T(8,128)(2,1)}, u32[]{:S(2)}) copy-start(bf16[2,4,48,1024]{3,2,1,0:T(8,128)(2,1)} %get-tuple-element.31) | copy-start | bytes 2359300
  253.8 309.4 %all-gather.4.cloned.1.call-start = ((), (), s32[]{:S(2)}) async-start(), calls=%async_computation.1 | async-start | bytes 9437184 | tf_op jit(solution)/shard_map/all_gather | solution.py:964
  339.7 248.7 %all-reduce.12.cloned.1.call-start = ((), (), s32[]{:S(2)}) async-start(), calls=%async_computation.2 | async-start | bytes 262144 | tf_op jit(solution)/shard_map/psum | solution.py:967
  430.5 14.6 %copy-start.15 = (u32[128]{0:T(128)S(1)}, u32[128]{0:T(128)}, u32[]{:S(2)}) copy-start(u32[128]{0:T(128)} %constant.57) | copy-start | bytes 1540
  430.5 26.2 %copy-start.11 = (f32[64,128]{1,0:T(8,128)S(1)}, f32[64,128]{1,0:T(8,128)}, u32[]{:S(2)}) copy-start(f32[64,128]{1,0:T(8,128)} %get-tuple-element.30) | copy-start | bytes 98308
  430.6 28.6 %copy-start.1 = (bf16[1024,1024]{1,0:T(8,128)(2,1)S(1)}, bf16[1024,1024]{1,0:T(8,128)(2,1)}, u32[]{:S(2)}) copy-start(bf16[1024,1024]{1,0:T(8,128)(2,1)} %get-tuple-element.28) | copy-start | bytes 6291460
  582.2 6.2 %copy-start.4 = (bf16[256,1024]{1,0:T(8,128)(2,1)S(1)}, bf16[256,1024]{1,0:T(8,128)(2,1)}, u32[]{:S(2)}) copy-start(bf16[256,1024]{1,0:T(8,128)(2,1)} %get-tuple-element.128) | copy-start | bytes 1572868
  582.2 7.0 %copy-start.3 = (bf16[256,1024]{1,0:T(8,128)(2,1)S(1)}, bf16[256,1024]{1,0:T(8,128)(2,1)}, u32[]{:S(2)}) copy-start(bf16[256,1024]{1,0:T(8,128)(2,1)} %get-tuple-element.129) | copy-start | bytes 1572868
  588.3 1.6 copy-start.6
Sparse Core Ops, SparseCore 0:
  254.0 85.6 all-reduce.9
  341.4 51.2 all-gather.3
Sparse Core Ops, SparseCore 1:
  345.5 167.1 all-reduce.11
